TPU v7x, 128 devices: a whole 4x4x4 slice. The times are simulated.
128 devices in a mesh: slab: 4 (over z), brick: 32 (over x, y, core).
Axes of the slice: x: 4, y: 4, z: 4, core: 2. Of those that a mesh axis runs over, the one named last changes fastest.
Arguments:
- grid_latent: bfloat16 [262144, 256], P(('slab', 'brick')), may hold values from -6 to 6
- mesh_node_latents: bfloat16 [196608, 256], P(('slab', 'brick')), may hold values from -6 to 6
- grid_cot: bfloat16 [262144, 256], P(('slab', 'brick')), may hold values from -6 to 6
- mesh_cotangent: bfloat16 [196608, 256], P(('slab', 'brick')), may hold values from -6 to 6
- w_first: bfloat16 [2, 512, 256], replicated, may hold values from -0.25 to 0.25
- w_second: bfloat16 [2, 256, 256], replicated, may hold values from -0.375 to 0.375
- biases: float32 [2, 256], replicated, may hold values from -3 to 3
- ln_gain: float32 [2, 256], replicated, may hold values from 0.5 to 1.5
- ln_shift: float32 [2, 256], replicated, may hold values from -3 to 3
- requests: int32 [16384, 8], P(('slab', 'brick')), may hold values from 0 to 1535
- counts: int32 [128, 128], P(('slab', 'brick')), may hold values from 1 to 8, as said below
- enc_slots: int32 [2, 262144], P(None, ('slab', 'brick')), may hold values from 0 to 1023, as said below
- dec_slots: int32 [3, 262144], P(None, ('slab', 'brick')), may hold values from 0 to 1023, as said below
Outputs:
- grid_grad: float32 [262144, 256], P(('slab', 'brick'))
- mesh_latent_gradient: float32 [196608, 256], P(('slab', 'brick'))
- w_first_grad: float32 [2, 512, 256], replicated
- w_second_grad: float32 [2, 256, 256], replicated
- bias_grad: float32 [2, 256], replicated
- gain_grad: float32 [2, 256], replicated
- shift_grad: float32 [2, 256], replicated
Inputs may be any that keep to these rules, and one draw needn't show every extreme that they name: `counts`: every device has a peer of which it asks all 8 slots, and that peer is the same for all devices. `requests`: entries of dead slots are rows too but are not read. `enc_slots`: each names a live slot p * 8 + c of its device, c < counts[r, p]. `dec_slots`: each names a live slot p * 8 + c of its device, c < counts[r, p].
All inputs are finite; a program needn't handle non-finite values.
Results may differ from a plain program's by a relative error of at most 0.0044.
Values may be sent and summed in bfloat16 or wider, within the bound.
A program may use at most 128 MiB of HBM per device.

v0:
```python
import math

import jax
import jax.numpy as jnp
from jax import lax
from jax.sharding import PartitionSpec as P

EPS = 1e-05


def edge_forward(inputs, first_layer, bias_row, second_layer, gain_row, shift_row):
    preact = jnp.dot(inputs, first_layer, preferred_element_type=jnp.float32) + bias_row
    hidden = jax.nn.silu(preact).astype(jnp.bfloat16)
    outer = jnp.dot(hidden, second_layer, preferred_element_type=jnp.float32)
    center = outer - jnp.mean(outer, axis=-1, keepdims=True)
    invstd = lax.rsqrt(jnp.mean(center * center, axis=-1, keepdims=True) + EPS)
    normed = center * invstd
    return (normed * gain_row + shift_row, (preact, hidden, normed, invstd))


def edge_backward(inputs, first_layer, second_layer, gain_row, stored, cotangent):
    preact, hidden, normed, invstd = stored
    gain_part = jnp.sum(cotangent * normed, axis=0)
    shift_part = jnp.sum(cotangent, axis=0)
    grad_normed = cotangent * gain_row
    outer_grad = invstd * (
        grad_normed
        - jnp.mean(grad_normed, axis=-1, keepdims=True)
        - normed * jnp.mean(grad_normed * normed, axis=-1, keepdims=True)
    )
    outer_low = outer_grad.astype(jnp.bfloat16)
    second_part = lax.dot_general(
        hidden, outer_low, (((0,), (0,)), ((), ())), preferred_element_type=jnp.float32
    )
    hidden_grad = lax.dot_general(
        outer_low, second_layer, (((1,), (1,)), ((), ())), preferred_element_type=jnp.float32
    )
    sigmoid_pre = jax.nn.sigmoid(preact)
    preact_grad = hidden_grad * sigmoid_pre * (1.0 + preact * (1.0 - sigmoid_pre))
    bias_part = jnp.sum(preact_grad, axis=0)
    preact_low = preact_grad.astype(jnp.bfloat16)
    first_part = lax.dot_general(
        inputs, preact_low, (((0,), (0,)), ((), ())), preferred_element_type=jnp.float32
    )
    input_grad = lax.dot_general(
        preact_low, first_layer, (((1,), (1,)), ((), ())), preferred_element_type=jnp.float32
    )
    return (input_grad, (first_part, second_part, bias_part, gain_part, shift_part))


def local_inputs(grid_rows, gathered_rows, slot_ids):
    fanout = slot_ids.shape[0]
    grid_tiled = jnp.tile(grid_rows, (fanout, 1))
    mesh_rows = jnp.take(gathered_rows, slot_ids.reshape(-1), axis=0)
    return jnp.concatenate([grid_tiled, mesh_rows], axis=1)


def per_device(
    grid_latent,
    mesh_node_latents,
    grid_cot,
    mesh_cotangent,
    w_first,
    w_second,
    biases,
    ln_gain,
    ln_shift,
    requests,
    counts,
    enc_slots,
    dec_slots,
):
    cell_count = grid_latent.shape[0]
    features = grid_latent.shape[1]
    mesh_count = mesh_node_latents.shape[0]
    peer_count = lax.axis_size(("slab", "brick"))
    capacity = requests.shape[1]
    slot_total = peer_count * capacity
    asked_rows, asked_count = (
        lax.all_to_all(requests, ("slab", "brick"), split_axis=0, concat_axis=0, tiled=True),
        lax.all_to_all(
            counts.reshape(peer_count, 1),
            ("slab", "brick"),
            split_axis=0,
            concat_axis=0,
            tiled=True,
        ),
    )
    live_in = lax.broadcasted_iota(jnp.int32, (peer_count, capacity), 1) < asked_count
    flat_asked = asked_rows.reshape(-1)
    live_flat = live_in.reshape(-1, 1)

    def serve(device_table):
        selected_rows = jnp.take(device_table, flat_asked, axis=0)
        selected_rows = jnp.where(live_flat, selected_rows, jnp.zeros_like(selected_rows))
        blocks = selected_rows.reshape(peer_count, capacity, features)
        arrived = lax.all_to_all(blocks, ("slab", "brick"), split_axis=0, concat_axis=0, tiled=True)
        return arrived.reshape(slot_total, features)

    def collect(partial_value):
        blocks = partial_value.reshape(peer_count, capacity, features)
        arrived = lax.all_to_all(blocks, ("slab", "brick"), split_axis=0, concat_axis=0, tiled=True)
        arrived = arrived.reshape(slot_total, features)
        arrived = jnp.where(live_flat, arrived, jnp.zeros_like(arrived))
        return jnp.zeros((mesh_count, features), jnp.float32).at[flat_asked].add(arrived)

    def slot_sums(slot_ids, values):
        return jnp.zeros((slot_total, features), jnp.float32).at[slot_ids.reshape(-1)].add(values)

    enc_fanout = enc_slots.shape[0]
    dec_fanout = dec_slots.shape[0]
    gathered_rows = serve(mesh_node_latents)
    enc_inputs = local_inputs(grid_latent, gathered_rows, enc_slots)
    enc_message, enc_stored = edge_forward(
        enc_inputs, w_first[0], biases[0], w_second[0], ln_gain[0], ln_shift[0]
    )
    enc_total = collect(slot_sums(enc_slots, enc_message))
    mesh_intermediate = (mesh_node_latents.astype(jnp.float32) + enc_total).astype(jnp.bfloat16)
    fetched_mid = serve(mesh_intermediate)
    dec_inputs = local_inputs(grid_latent, fetched_mid, dec_slots)
    dec_message, dec_stored = edge_forward(
        dec_inputs, w_first[1], biases[1], w_second[1], ln_gain[1], ln_shift[1]
    )
    dec_cot = jnp.tile(grid_cot.astype(jnp.float32), (dec_fanout, 1))
    dec_grad, dec_parts = edge_backward(
        dec_inputs, w_first[1], w_second[1], ln_gain[1], dec_stored, dec_cot
    )
    mesh_intermediate_gradient = mesh_cotangent.astype(jnp.float32) + collect(
        slot_sums(dec_slots, dec_grad[:, features:])
    )
    gathered_row_gradient = serve(mesh_intermediate_gradient.astype(jnp.bfloat16))
    enc_cot = jnp.take(gathered_row_gradient, enc_slots.reshape(-1), axis=0).astype(jnp.float32)
    enc_grad, enc_parts = edge_backward(
        enc_inputs, w_first[0], w_second[0], ln_gain[0], enc_stored, enc_cot
    )
    mesh_latent_gradient = mesh_intermediate_gradient + collect(
        slot_sums(enc_slots, enc_grad[:, features:])
    )
    dec_grid = dec_grad[:, :features].reshape(dec_fanout, cell_count, features).sum(axis=0)
    enc_grid = enc_grad[:, :features].reshape(enc_fanout, cell_count, features).sum(axis=0)
    grid_grad = grid_cot.astype(jnp.float32) + dec_grid + enc_grid
    stacked = tuple((jnp.stack([enc_parts[index], dec_parts[index]]) for index in range(5)))
    summed = lax.psum(
        (stacked[0], stacked[1], stacked[2], stacked[3], stacked[4]), ("slab", "brick")
    )
    enc_scale = 1.0 / math.sqrt(enc_fanout * cell_count * peer_count)
    dec_scale = 1.0 / math.sqrt(dec_fanout * cell_count * peer_count)
    results = [
        jnp.stack([summed[index][0] * enc_scale, summed[index][1] * dec_scale])
        for index in range(5)
    ]
    return (
        grid_grad,
        mesh_latent_gradient,
        results[0],
        results[1],
        results[2],
        results[3],
        results[4],
    )


def solution(mesh):
    return jax.shard_map(
        per_device,
        mesh=mesh,
        in_specs=(
            P(("slab", "brick"), None),
            P(("slab", "brick"), None),
            P(("slab", "brick"), None),
            P(("slab", "brick"), None),
            P(),
            P(),
            P(),
            P(),
            P(),
            P(("slab", "brick"), None),
            P(("slab", "brick"), None),
            P(None, ("slab", "brick")),
            P(None, ("slab", "brick")),
        ),
        out_specs=(P(("slab", "brick"), None), P(("slab", "brick"), None), P(), P(), P(), P(), P()),
        check_vma=False,
    )
```

profile of v0, /device:TPU:1, one launch (start us, length us, event | category | flops | bytes accessed | tf_op | source)
XLA Modules:
  0.0 668.3 jit_solution(1984406883587997508)
XLA Ops:
  8.7 11.5 %all-to-all-start = ((s32[128,1,1]{2,1,0:T(1,128)}), s32[128,1,1]{2,1,0:T(1,128)S(1)}, u32[]{:S(2)}, u32[]{:S(2)}) async-start(s32[128,1,1]{2,1,0:T(1,128)} %copy.40), calls=%async_computation | async-start | bytes 131072 | tf_op jit(solution)/shard_map/all_to_all | solution.py:81
  25.0 4.7 all-to-all-done
  29.7 5.1 all-to-all-start.1
  37.3 7.0 %all-to-all-done.1 = s32[128,1,8]{2,1,0:T(1,128)S(1)} async-done(((s32[128,1,8]{2,1,0:T(1,128)}), s32[128,1,8]{2,1,0:T(1,128)S(1)}, u32[]{:S(2)}, u32[]{:S(2)}) %all-to-all-start.1) | async-done | bytes 4128 | tf_op jit(solution)/shard_map/all_to_all | solution.py:80
  45.8 4.7 gather_fusion.1
  51.6 4.7 all-to-all-start.2
  61.1 8.6 %all-to-all-done.2 = bf16[128,8,256]{2,1,0:T(8,128)(2,1)S(1)} async-done(((bf16[128,8,256]{2,1,0:T(8,128)(2,1)}), bf16[128,8,256]{2,1,0:T(8,128)(2,1)S(1)}, u32[]{:S(2)}, u32[]{:S(2)}) %all-to-all-start.2) | async-done | bytes 524320 | tf_op jit(solution)/shard_map/all_to_all | solution.py:97
  69.7 17.0 %gather_fusion.2 = bf16[4096,256]{1,0:T(8,128)(2,1)} fusion(bf16[1024,256]{1,0:T(8,128)(2,1)S(1)} %bitcast.107, s32[4096]{0:T(1024)S(1)} %fusion.60), kind=kCustom, calls=%fused_computation.1.clone | custom fusion | bytes 4210688 | tf_op jit(solution)/shard_map/jit(_take)/gather | solution.py:54
  89.0 3.1 multiply_convert_fusion.2
  95.6 2.7 multiply_add_fusion
  98.3 5.7 copy.42
  104.0 23.8 %scatter_custom_fusion = f32[1024,256]{1,0:T(8,128)} fusion(s32[4096]{0:T(1024)} %bitcast.133, f32[4096,256]{1,0:T(8,128)} %copy.42, f32[]{:T(128)} %constant.34.clone.1), kind=kCustom, calls=%fused_computation.88 | custom fusion | flops 1048576 | bytes 1049088 | tf_op jit(solution)/shard_map/scatter-add | solution.py:108
  127.8 4.6 all-to-all-start.3
  133.1 18.2 %all-to-all-done.3 = f32[128,8,256]{2,1,0:T(8,128)S(1)} async-done(((f32[128,8,256]{2,1,0:T(8,128)}), f32[128,8,256]{2,1,0:T(8,128)S(1)}, u32[]{:S(2)}, u32[]{:S(2)}) %all-to-all-start.3) | async-done | bytes 1048608 | tf_op jit(solution)/shard_map/all_to_all | solution.py:102
  151.3 9.1 %scatter_custom_fusion.1 = f32[1536,256]{1,0:T(8,128)} fusion(f32[1536,256]{1,0:T(8,128)} %convert_element_type.38, s32[1024]{0:T(1024)S(1)} %bitcast.141, f32[128,8,256]{2,1,0:T(8,128)S(1)} %all-to-all-done.3, f32[]{:T(128)} %constant.34.clone.1, pred[1024]{0:T(1024)(128)(4,1)S(1)} %copy-done.33), kind=kCustom, calls=%fused_computation.69 | custom fusion | flops 524288 | bytes 2622976 | tf_op jit(solution)/shard_map/scatter-add | solution.py:105
  162.0 4.4 gather_fusion.3
  167.6 5.1 all-to-all-start.4
  172.8 4.4 tile.33
  177.1 6.6 copy.43
  186.3 25.1 %gather_fusion = bf16[6144,256]{1,0:T(8,128)(2,1)} fusion(bf16[1024,256]{1,0:T(8,128)(2,1)S(1)} %bitcast.105, s32[6144]{0:T(1024)S(1)} %broadcast_clamp_fusion), kind=kCustom, calls=%fused_computation.5 | custom fusion | bytes 6316032 | tf_op jit(solution)/shard_map/jit(_take)/gather | solution.py:54
  211.4 4.8 broadcast_select_fusion
  216.5 4.5 multiply_convert_fusion.1
  225.0 2.7 multiply_reduce_fusion
  227.7 3.4 multiply_convert_fusion
  231.1 6.2 fusion.70
  239.0 6.4 fusion.17
  245.4 35.3 %scatter_custom_fusion.2 = f32[1024,256]{1,0:T(8,128)} fusion(s32[6144]{0:T(1024)S(1)} %bitcast.125, f32[6144,512]{1,0:T(8,128)} %fusion.17, f32[]{:T(128)} %constant.34.clone.1), kind=kCustom, calls=%fused_computation.15 | custom fusion | flops 1572864 | bytes 7340544 | tf_op jit(solution)/shard_map/scatter-add | solution.py:108
  280.6 7.4 %all-to-all-start.5 = ((f32[128,8,256]{2,1,0:T(8,128)}), f32[128,8,256]{2,1,0:T(8,128)S(1)}, u32[]{:S(2)}, u32[]{:S(2)}) async-start(f32[128,8,256]{2,1,0:T(8,128)} %bitcast.115), calls=%async_computation.5 | async-start | bytes 2097152 | tf_op jit(solution)/shard_map/all_to_all | solution.py:102
  291.2 15.7 %all-to-all-done.5 = f32[128,8,256]{2,1,0:T(8,128)S(1)} async-done(((f32[128,8,256]{2,1,0:T(8,128)}), f32[128,8,256]{2,1,0:T(8,128)S(1)}, u32[]{:S(2)}, u32[]{:S(2)}) %all-to-all-start.5) | async-done | bytes 1048608 | tf_op jit(solution)/shard_map/all_to_all | solution.py:102
  306.9 9.3 %scatter_custom_fusion.3 = f32[1536,256]{1,0:T(8,128)} fusion(f32[1536,256]{1,0:T(8,128)} %convert_element_type.44, s32[1024]{0:T(1024)} %bitcast.142, f32[128,8,256]{2,1,0:T(8,128)S(1)} %all-to-all-done.5, f32[]{:T(128)} %constant.34.clone.1, pred[1024]{0:T(1024)(128)(4,1)S(1)} %copy-done.35), kind=kCustom, calls=%fused_computation.67 | custom fusion | flops 524288 | bytes 2622976 | tf_op jit(solution)/shard_map/scatter-add | solution.py:105
  317.7 3.9 gather_fusion.4
  322.8 4.7 all-to-all-start.6
  327.4 6.4 fusion.19
  333.9 5.8 slice.109
  339.6 4.8 reduce_sum.150
  344.4 4.6 convolution_bitcast_fusion
  349.0 17.0 %gather_fusion.5 = bf16[4096,256]{1,0:T(8,128)(2,1)} fusion(bf16[1024,256]{1,0:T(8,128)(2,1)S(1)} %bitcast.106, s32[4096]{0:T(1024)S(1)} %fusion.60), kind=kCustom, calls=%fused_computation.4.clone | custom fusion | bytes 4210688 | tf_op jit(solution)/shard_map/jit(_take)/gather | solution.py:132
  366.1 3.1 copy.44
  369.2 4.7 fusion.11
  382.1 4.5 fusion.27
  386.6 24.2 %scatter_custom_fusion.4 = f32[1024,256]{1,0:T(8,128)} fusion(s32[4096]{0:T(1024)} %bitcast.134, f32[4096,512]{1,0:T(8,128)} %fusion.27, f32[]{:T(128)} %constant.34.clone.1), kind=kCustom, calls=%fused_computation.40 | custom fusion | flops 1048576 | bytes 5243392 | tf_op jit(solution)/shard_map/scatter-add | solution.py:108
  410.8 4.4 slice.111
  415.3 67.7 %all-reduce = (f32[2,256]{1,0:T(2,128)S(1)}, f32[2,256]{1,0:T(2,128)S(1)}, f32[2,256]{1,0:T(2,128)S(1)}) all-reduce(f32[2,256]{1,0:T(2,128)S(1)} %pad_maximum_fusion.14, f32[2,256]{1,0:T(2,128)S(1)} %get-tuple-element.48, f32[2,256]{1,0:T(2,128)S(1)} %get-tuple-element.49), channel_id=1, replica_groups=mesh['slab'=4,'brick'=32] {'slab','brick'}, use_global_device_ids=true, to_apply=%region_20.23 | all-reduce | flops 1536 | bytes 12288 | tf_op jit(solution)/shard_map/psum | solution.py:143
  483.0 2.7 reduce_sum.153
  485.7 5.5 all-to-all-start.7
  495.3 3.2 add_add_fusion
  500.3 147.7 %all-reduce.4.cloned.1.call-done = (f32[2,512,256]{2,1,0:T(8,128)}, f32[2,256,256]{2,1,0:T(8,128)}) async-done(((f32[2,512,256]{2,1,0:T(8,128)}, f32[2,256,256]{2,1,0:T(8,128)}), (f32[2,512,256]{2,1,0:T(8,128)}, f32[2,256,256]{2,1,0:T(8,128)})) %all-reduce.4.cloned.1.call-update) | async-done | bytes 1572880 | tf_op jit(solution)/shard_map/psum | solution.py:143
  652.3 7.7 %scatter_custom_fusion.5 = f32[1536,256]{1,0:T(8,128)S(1)} fusion(f32[1536,256]{1,0:T(8,128)S(1)} %copy-done.7, s32[1024]{0:T(1024)} %bitcast.143, f32[128,8,256]{2,1,0:T(8,128)} %all-to-all-done.7, f32[]{:T(128)} %constant.34.clone.1, pred[1024]{0:T(1024)(128)(4,1)S(1)} %copy-done.35), kind=kCustom, calls=%fused_computation.65 | custom fusion | flops 524288 | bytes 2622976 | tf_op jit(solution)/shard_map/scatter-add | solution.py:105
  (173 shorter events, 58.9 us)
Async XLA Ops:
  7.2 49.7 %copy-start.2 = (bf16[1536,256]{1,0:T(8,128)(2,1)S(1)}, bf16[1536,256]{1,0:T(8,128)(2,1)}, u32[]{:S(2)}) copy-start(bf16[1536,256]{1,0:T(8,128)(2,1)} %param.18) | copy-start | bytes 2359300
  7.2 49.1 %copy-start.44 = (f32[2,256]{1,0:T(2,128)S(1)}, f32[2,256]{1,0:T(2,128)}, u32[]{:S(2)}) copy-start(f32[2,256]{1,0:T(2,128)} %param.24) | copy-start | bytes 6148
  8.7 21.0 %all-to-all-start = ((s32[128,1,1]{2,1,0:T(1,128)}), s32[128,1,1]{2,1,0:T(1,128)S(1)}, u32[]{:S(2)}, u32[]{:S(2)}) async-start(s32[128,1,1]{2,1,0:T(1,128)} %copy.40), calls=%async_computation | async-start | bytes 131072 | tf_op jit(solution)/shard_map/all_to_all | solution.py:81
  22.3 64.5 %copy-start.28 = (pred[4096]{0:T(1024)(128)(4,1)}, pred[4096]{0:T(1024)(128)(4,1)S(1)}, u32[]{:S(2)}) copy-start(pred[4096]{0:T(1024)(128)(4,1)S(1)} %compare_and_fusion.1) | copy-start | bytes 12292
  29.7 14.6 %all-to-all-start.1 = ((s32[128,1,8]{2,1,0:T(1,128)}), s32[128,1,8]{2,1,0:T(1,128)S(1)}, u32[]{:S(2)}, u32[]{:S(2)}) async-start(s32[128,1,8]{2,1,0:T(1,128)} %bitcast.2), calls=%async_computation.1 | async-start | bytes 131072 | tf_op jit(solution)/shard_map/all_to_all | solution.py:80
  37.3 20.8 %copy-start.32 = (pred[1024]{0:T(1024)(128)(4,1)}, pred[1024]{0:T(1024)(128)(4,1)S(1)}, u32[]{:S(2)}) copy-start(pred[1024]{0:T(1024)(128)(4,1)S(1)} %lt.80) | copy-start | bytes 3076
  45.7 12.4 %copy-start.38 = (pred[1024]{0:T(1024)(128)(4,1)}, pred[1024]{0:T(1024)(128)(4,1)S(1)}, u32[]{:S(2)}) copy-start(pred[1024]{0:T(1024)(128)(4,1)S(1)} %compare_and_fusion.2) | copy-start | bytes 3076
  45.8 12.4 %copy-start.30 = (s32[1024]{0:T(1024)}, s32[1024]{0:T(1024)S(1)}, u32[]{:S(2)}) copy-start(s32[1024]{0:T(1024)S(1)} %fusion.61) | copy-start | bytes 12292
  45.8 12.4 %copy-start.24 = (s32[3,2048]{1,0:T(4,128)S(1)}, s32[3,2048]{1,0:T(4,128)}, u32[]{:S(2)}) copy-start(s32[3,2048]{1,0:T(4,128)} %param.29) | copy-start | bytes 73732
  51.6 18.1 %all-to-all-start.2 = ((bf16[128,8,256]{2,1,0:T(8,128)(2,1)}), bf16[128,8,256]{2,1,0:T(8,128)(2,1)S(1)}, u32[]{:S(2)}, u32[]{:S(2)}) async-start(bf16[128,8,256]{2,1,0:T(8,128)(2,1)} %fusion.31), calls=%async_computation.2 | async-start | bytes 1048576 | tf_op jit(solution)/shard_map/all_to_all | solution.py:97
  56.9 29.9 %copy-start.36 = (f32[1,256]{1,0:T(1,128)}, f32[1,256]{1,0:T(1,128)S(1)}, u32[]{:S(2)}) copy-start(f32[1,256]{1,0:T(1,128)S(1)} %get-tuple-element.30) | copy-start | bytes 3076
  86.8 2.1 copy-start.9
  86.8 2.3 copy-start.18
  88.8 3.3 copy-start.14
  89.0 3.2 copy-start.16
  89.0 3.1 copy-start.21
  98.3 34.1 %copy-start.27 = (s32[1,1,3,2048]{3,1,2,0:T(1,128)S(1)}, s32[1,1,3,2048]{3,1,2,0:T(1,128)}, u32[]{:S(2)}) copy-start(s32[1,1,3,2048]{3,1,2,0:T(1,128)} %copy.48) | copy-start | bytes 73732
  98.3 53.0 %copy-start.33 = (pred[1024]{0:T(1024)(128)(4,1)S(1)}, pred[1024]{0:T(1024)(128)(4,1)}, u32[]{:S(2)}) copy-start(pred[1024]{0:T(1024)(128)(4,1)} %copy-done.32) | copy-start | bytes 3076
  127.8 23.5 %all-to-all-start.3 = ((f32[128,8,256]{2,1,0:T(8,128)}), f32[128,8,256]{2,1,0:T(8,128)S(1)}, u32[]{:S(2)}, u32[]{:S(2)}) async-start(f32[128,8,256]{2,1,0:T(8,128)} %bitcast.113), calls=%async_computation.3 | async-start | bytes 2097152 | tf_op jit(solution)/shard_map/all_to_all | solution.py:102
  133.1 27.4 %copy-start.43 = (s32[1024,1]{0,1:T(1,128)}, s32[1024,1]{0,1:T(1,128)S(1)}, u32[]{:S(2)}) copy-start(s32[1024,1]{0,1:T(1,128)S(1)} %compare_select_fusion.4) | copy-start | bytes 12292
  160.5 6.0 copy-start.34
  160.5 6.0 copy-start.39
  160.5 12.2 %copy-start.25 = (s32[3,2048]{1,0:T(4,128)S(1)}, s32[3,2048]{1,0:T(4,128)}, u32[]{:S(2)}) copy-start(s32[3,2048]{1,0:T(4,128)} %param.29) | copy-start | bytes 73732
  167.6 18.7 %all-to-all-start.4 = ((bf16[128,8,256]{2,1,0:T(8,128)(2,1)}), bf16[128,8,256]{2,1,0:T(8,128)(2,1)S(1)}, u32[]{:S(2)}, u32[]{:S(2)}) async-start(bf16[128,8,256]{2,1,0:T(8,128)(2,1)} %fusion.30), calls=%async_computation.4 | async-start | bytes 1048576 | tf_op jit(solution)/shard_map/all_to_all | solution.py:97
  177.1 6.6 copy-start.26
  211.4 4.8 copy-start.10
  211.4 5.0 copy-start.19
  211.4 5.1 copy-start.45
  216.2 4.8 copy-start.12
  216.4 4.5 copy-start.13
  216.5 4.5 copy-start.22
  221.0 3.3 slice-start
  221.0 4.0 slice-start.1
  222.8 2.2 copy-start.37
  280.6 26.3 %copy-start.35 = (pred[1024]{0:T(1024)(128)(4,1)S(1)}, pred[1024]{0:T(1024)(128)(4,1)}, u32[]{:S(2)}) copy-start(pred[1024]{0:T(1024)(128)(4,1)} %copy-done.32) | copy-start | bytes 3076
  280.6 26.3 %all-to-all-start.5 = ((f32[128,8,256]{2,1,0:T(8,128)}), f32[128,8,256]{2,1,0:T(8,128)S(1)}, u32[]{:S(2)}, u32[]{:S(2)}) async-start(f32[128,8,256]{2,1,0:T(8,128)} %bitcast.115), calls=%async_computation.5 | async-start | bytes 2097152 | tf_op jit(solution)/shard_map/all_to_all | solution.py:102
  288.0 29.7 %copy-start.31 = (s32[1024]{0:T(1024)S(1)}, s32[1024]{0:T(1024)}, u32[]{:S(2)}) copy-start(s32[1024]{0:T(1024)} %copy-done.30) | copy-start | bytes 12292
  316.2 5.5 copy-start.40
  322.8 26.2 %all-to-all-start.6 = ((bf16[128,8,256]{2,1,0:T(8,128)(2,1)}), bf16[128,8,256]{2,1,0:T(8,128)(2,1)S(1)}, u32[]{:S(2)}, u32[]{:S(2)}) async-start(bf16[128,8,256]{2,1,0:T(8,128)(2,1)} %fusion.29), calls=%async_computation.6 | async-start | bytes 1048576 | tf_op jit(solution)/shard_map/all_to_all | solution.py:97
  366.1 3.1 copy-start.29
  366.1 3.2 copy-start.42
  369.2 4.7 copy-start.1
  375.5 2.3 copy-start.46
  377.8 2.2 copy-start.17
  485.7 9.6 %copy-start.5 = (bf16[2048,256]{1,0:T(8,128)(2,1)S(1)}, bf16[2048,256]{1,0:T(8,128)(2,1)}, u32[]{:S(2)}) copy-start(bf16[2048,256]{1,0:T(8,128)(2,1)} %param.19) | copy-start | bytes 3145732
  485.7 166.6 %all-to-all-start.7 = ((f32[128,8,256]{2,1,0:T(8,128)}), f32[128,8,256]{2,1,0:T(8,128)}, u32[]{:S(2)}, u32[]{:S(2)}) async-start(f32[128,8,256]{2,1,0:T(8,128)} %bitcast.114), calls=%async_computation.7 | async-start | bytes 2097152 | tf_op jit(solution)/shard_map/all_to_all | solution.py:102
  491.2 156.9 %all-reduce.4.cloned.1.call-start = ((), (), s32[]{:S(2)}) async-start(), calls=%async_computation.8 | async-start | bytes 3145728 | tf_op jit(solution)/shard_map/psum | solution.py:143
  498.6 153.8 %copy-start.7 = (f32[1536,256]{1,0:T(8,128)S(1)}, f32[1536,256]{1,0:T(8,128)}, u32[]{:S(2)}) copy-start(f32[1536,256]{1,0:T(8,128)} %scatter_custom_fusion.3) | copy-start | bytes 4718596
  (11 other events, 18.6 us)
Sparse Core Ops, SparseCore 0:
  497.4 150.5 all-reduce.3
where the time goes:
time: 674 us; the launch traced here: 668 us
  waiting for transfers between devices  204 us (30%)
  other arithmetic  171 us (25%)
  local copies, waits for them, and re-layouts  119 us (18%)
  blocking collectives  67.7 us (10%)
  starting transfers between devices  48.5 us (7%)
  matrix products  42.4 us (6%)
  between operations  15 us (2%)
    psum x1, waiting for transfers between devices, per_device(): lax.psum((stacked[0], stacked[1], stacked[2], stacked[3], stacked[4]), ('...  148 us
    scatter-add x3, other arithmetic, slot_sums(): jnp.zeros((slot_total, features), jnp.float32).at[slot_ids.reshape(-1)]  83.3 us
    psum x1, blocking collectives, per_device(): lax.psum((stacked[0], stacked[1], stacked[2], stacked[3], stacked[4]), ('...  67.7 us
    gather x2, local copies, waits for them, and re-layouts, local_inputs(): mesh_rows = jnp.take(gathered_rows, slot_ids.reshape(-1), axis=0)  42.1 us
    all_to_all x3, waiting for transfers between devices, collect(): lax.all_to_all(blocks, ('slab', 'brick'), split_axis=0, concat_axis=0, ti...  33.9 us
    scatter-add x3, other arithmetic, collect(): jnp.zeros((mesh_count, features), jnp.float32).at[flat_asked].add(arrived)  26.1 us
    gather x2, local copies, waits for them, and re-layouts, per_device(): jnp.take(gathered_row_gradient, enc_slots.reshape(-1), axis=0)  20.2 us
    all_to_all x3, starting transfers between devices, collect(): lax.all_to_all(blocks, ('slab', 'brick'), split_axis=0, concat_axis=0, ti...  17.4 us
  transfers between devices with their start and end apart: 9, of which 7 were waited for; matrix products, arithmetic and copies ran while one was open for 9% of the time, Pallas kernels for 0%

commit v1 on v0

--- a/solution.py
+++ b/solution.py
@@ -1,11 +1,73 @@
+import functools
 import math
 
 import jax
 import jax.numpy as jnp
 from jax import lax
+from jax.experimental import pallas as pl
+from jax.experimental.pallas import tpu as pltpu
 from jax.sharding import PartitionSpec as P
 
 EPS = 1e-05
+
+
+def exchange_kernel(slabs, bricks, src_ref, out_ref, send_sem, recv_sem):
+    peers = slabs * bricks
+    me = lax.axis_index("slab") * bricks + lax.axis_index("brick")
+    barrier = pltpu.get_barrier_semaphore()
+
+    def greet(step, carry):
+        peer = lax.rem(me + step, peers)
+        pl.semaphore_signal(
+            barrier,
+            inc=1,
+            device_id=(peer // bricks, lax.rem(peer, bricks)),
+            device_id_type=pl.DeviceIdType.MESH,
+        )
+        return carry
+
+    lax.fori_loop(1, peers, greet, 0)
+    pl.semaphore_wait(barrier, peers - 1)
+
+    def send(step, carry):
+        peer = lax.rem(me + step, peers)
+        pltpu.make_async_remote_copy(
+            src_ref=src_ref.at[peer],
+            dst_ref=out_ref.at[me],
+            send_sem=send_sem,
+            recv_sem=recv_sem,
+            device_id=(peer // bricks, lax.rem(peer, bricks)),
+            device_id_type=pl.DeviceIdType.MESH,
+        ).start()
+        return carry
+
+    lax.fori_loop(1, peers, send, 0)
+    out_ref[me] = src_ref[me]
+    others = out_ref.at[pl.ds(0, peers - 1)]
+    pltpu.make_async_copy(others, others, send_sem).wait()
+    pltpu.make_async_copy(others, others, recv_sem).wait()
+
+
+def exchange(blocks, collective_id):
+    slabs, bricks = lax.axis_size("slab"), lax.axis_size("brick")
+    return pl.pallas_call(
+        functools.partial(exchange_kernel, slabs, bricks),
+        out_shape=jax.ShapeDtypeStruct(blocks.shape, blocks.dtype),
+        in_specs=[pl.BlockSpec(memory_space=pltpu.VMEM)],
+        out_specs=pl.BlockSpec(memory_space=pltpu.VMEM),
+        scratch_shapes=[pltpu.SemaphoreType.DMA, pltpu.SemaphoreType.DMA],
+        compiler_params=pltpu.CompilerParams(
+            collective_id=collective_id, has_side_effects=True, vmem_limit_bytes=16 << 20
+        ),
+    )(blocks)
+
+
+def exchange_rows(rows, peer_count, capacity):
+    half = rows.shape[1] // 2
+    blocks = rows.reshape(peer_count, capacity, 2, half).swapaxes(1, 2)
+    arrived = exchange(blocks.reshape(peer_count, 2 * capacity, half), 1)
+    arrived = arrived.reshape(peer_count, 2, capacity, half).swapaxes(1, 2)
+    return arrived.reshape(peer_count * capacity, 2 * half)
 
 
 def edge_forward(inputs, first_layer, bias_row, second_layer, gain_row, shift_row):
@@ -76,31 +138,23 @@
     peer_count = lax.axis_size(("slab", "brick"))
     capacity = requests.shape[1]
     slot_total = peer_count * capacity
-    asked_rows, asked_count = (
-        lax.all_to_all(requests, ("slab", "brick"), split_axis=0, concat_axis=0, tiled=True),
-        lax.all_to_all(
-            counts.reshape(peer_count, 1),
-            ("slab", "brick"),
-            split_axis=0,
-            concat_axis=0,
-            tiled=True,
-        ),
-    )
-    live_in = lax.broadcasted_iota(jnp.int32, (peer_count, capacity), 1) < asked_count
+    positions = lax.broadcasted_iota(jnp.int32, (peer_count, capacity), 1)
+    marked = jnp.where(positions < counts.reshape(peer_count, 1), requests, -1)
+    marked = jnp.broadcast_to(marked[:, :, None], (peer_count, capacity, 128))
+    marked = exchange(marked, 2)[:, :, 0]
+    asked_rows = jnp.maximum(marked, 0)
+    live_in = marked >= 0
     flat_asked = asked_rows.reshape(-1)
     live_flat = live_in.reshape(-1, 1)
 
     def serve(device_table):
         selected_rows = jnp.take(device_table, flat_asked, axis=0)
         selected_rows = jnp.where(live_flat, selected_rows, jnp.zeros_like(selected_rows))
-        blocks = selected_rows.reshape(peer_count, capacity, features)
-        arrived = lax.all_to_all(blocks, ("slab", "brick"), split_axis=0, concat_axis=0, tiled=True)
-        return arrived.reshape(slot_total, features)
+        return exchange_rows(selected_rows, peer_count, capacity)
 
     def collect(partial_value):
-        blocks = partial_value.reshape(peer_count, capacity, features)
-        arrived = lax.all_to_all(blocks, ("slab", "brick"), split_axis=0, concat_axis=0, tiled=True)
-        arrived = arrived.reshape(slot_total, features)
+        low = partial_value.astype(jnp.bfloat16)
+        arrived = exchange_rows(low, peer_count, capacity).astype(jnp.float32)
         arrived = jnp.where(live_flat, arrived, jnp.zeros_like(arrived))
         return jnp.zeros((mesh_count, features), jnp.float32).at[flat_asked].add(arrived)
 

time: 674 us -> 535 us (0.79)
  waiting for transfers between devices: 204 us -> 3.56 us
  Pallas kernels: 0 us -> 115 us
  starting transfers between devices: 48.5 us -> 0.04 us
    psum x1, waiting for transfers between devices: 148 us -> 3.54 us  [per_device(): lax.psum((stacked[0], stacked[1], stacked[2], stacked[3], stacked[4]), ('...]
    pallas_call x0 -> x7, Pallas kernels: none -> 115 us  [exchange(): pl.pallas_call(functools.partial(exchange_kernel, slabs, bricks), out_sha...]
    all_to_all x8 -> x0, waiting for transfers between devices: 56.7 us -> none  [the longest x3 33.9 us: collect(): lax.all_to_all(blocks, ('slab', 'brick'), split_axis=0, concat_axis=0, ti...]
    all_to_all x8 -> x0, starting transfers between devices: 48.4 us -> none  [the longest x3 17.4 us: collect(): lax.all_to_all(blocks, ('slab', 'brick'), split_axis=0, concat_axis=0, ti...]
  transfers between devices with their start and end apart: 9 -> 1, of which waited for: 7 -> 1; matrix products, arithmetic and copies ran while one was open for 9% -> 12% of each run, Pallas kernels for 0% -> 3%
where the time goes in v1:
time: 535 us; the launch traced here: 525 us
  other arithmetic  174 us (33%)
  Pallas kernels  115 us (21%)
  local copies, waits for them, and re-layouts  114 us (21%)
  blocking collectives  65.1 us (12%)
  matrix products  38.5 us (7%)
  between operations  14.9 us (3%)
    pallas_call x7, Pallas kernels, exchange(): pl.pallas_call(functools.partial(exchange_kernel, slabs, bricks), out_sha...  115 us
    scatter-add x3, other arithmetic, slot_sums(): jnp.zeros((slot_total, features), jnp.float32).at[slot_ids.reshape(-1)]  82.5 us
    psum x1, blocking collectives, per_device(): lax.psum((stacked[0], stacked[1], stacked[2], stacked[3], stacked[4]), ('...  65.1 us
    gather x2, local copies, waits for them, and re-layouts, local_inputs(): mesh_rows = jnp.take(gathered_rows, slot_ids.reshape(-1), axis=0)  41.9 us
    scatter-add x3, other arithmetic, collect(): jnp.zeros((mesh_count, features), jnp.float32).at[flat_asked].add(arrived)  27.5 us
    gather x2, local copies, waits for them, and re-layouts, per_device(): jnp.take(gathered_row_gradient, enc_slots.reshape(-1), axis=0)  21.1 us
    dot_general x2, matrix products, edge_backward(): lax.dot_general(preact_low, first_layer, (((1,), (1,)), ((), ())), prefer...  12.5 us
    gather x3, local copies, waits for them, and re-layouts, serve(): selected_rows = jnp.take(device_table, flat_asked, axis=0)  12.2 us
  transfers between devices with their start and end apart: 1, of which 1 were waited for; matrix products, arithmetic and copies ran while one was open for 12% of the time, Pallas kernels for 3%

profile of v1, /device:TPU:1, one launch (start us, length us, event | category | flops | bytes accessed | tf_op | source)
XLA Modules:
  0.0 525.3 jit_solution(9268665261121028931)
XLA Ops:
  9.0 20.4 %shard_map.180 = s32[128,8,128]{2,1,0:T(8,128)S(1)} custom-call(s32[128,8,128]{2,1,0:T(8,128)S(1)} %broadcast_in_dim.80.src_ref), custom_call_target="tpu_custom_call" | custom-call | tf_op jit(solution)/shard_map/pallas_call | solution.py:53
  29.5 2.3 compare_reduce_fusion
  31.7 2.2 maximum_reduce_fusion
  38.7 2.4 convert_element_type.83
  41.1 3.9 gather_fusion.1
  45.4 15.6 %shard_map.181 = bf16[128,16,128]{2,1,0:T(8,128)(2,1)S(1)} custom-call(bf16[128,16,128]{2,1,0:T(8,128)(2,1)S(1)} %fusion.37.src_ref), custom_call_target="tpu_custom_call" | custom-call | tf_op jit(solution)/shard_map/pallas_call | solution.py:53
  63.4 17.0 %gather_fusion.2 = bf16[4096,256]{1,0:T(8,128)(2,1)} fusion(bf16[1024,256]{1,0:T(8,128)(2,1)S(1)} %bitcast.166, s32[4096]{0:T(1024)S(1)} %fusion.66), kind=kCustom, calls=%fused_computation.1.clone | custom fusion | bytes 4210688 | tf_op jit(solution)/shard_map/jit(_take)/gather | solution.py:116
  80.5 2.1 broadcast_select_fusion.1
  82.7 3.1 multiply_convert_fusion.2
  89.0 2.7 multiply_add_fusion
  91.7 5.6 %copy.29 = f32[4096,256]{1,0:T(8,128)} copy(f32[4096,256]{0,1:T(8,128)} %multiply_add_fusion) | data formatting | bytes 8388608 | tf_op jit(solution)/shard_map/add | solution.py:80
  97.3 24.0 %scatter_custom_fusion = f32[1024,256]{1,0:T(8,128)} fusion(s32[4096]{0:T(1024)S(1)} %bitcast.189, f32[4096,256]{1,0:T(8,128)} %copy.29, f32[]{:T(128)} %constant.27.clone.1), kind=kCustom, calls=%fused_computation.97 | custom fusion | flops 1048576 | bytes 1049088 | tf_op jit(solution)/shard_map/scatter-add | solution.py:162
  122.6 16.0 %shard_map.182 = bf16[128,16,128]{2,1,0:T(8,128)(2,1)S(1)} custom-call(bf16[128,16,128]{2,1,0:T(8,128)(2,1)S(1)} %convert_bitcast_fusion.2.src_ref), custom_call_target="tpu_custom_call" | custom-call | tf_op jit(solution)/shard_map/pallas_call | solution.py:53
  138.6 9.1 %scatter_custom_fusion.1 = f32[1536,256]{1,0:T(8,128)} fusion(f32[1536,256]{1,0:T(8,128)} %convert_element_type.83, s32[1024]{0:T(1024)S(1)} %reshape.359, bf16[128,16,128]{2,1,0:T(8,128)(2,1)S(1)} %shard_map.182, f32[]{:T(128)} %constant.27.clone.1, pred[1024]{0:T(1024)(128)(4,1)S(1)} %ge.31), kind=kCustom, calls=%fused_computation.71 | custom fusion | flops 786432 | bytes 2098688 | tf_op jit(solution)/shard_map/scatter-add | solution.py:159
  147.8 1.5 convert_element_type.90
  149.2 3.9 gather_fusion.3
  154.2 16.1 %shard_map.183 = bf16[128,16,128]{2,1,0:T(8,128)(2,1)S(1)} custom-call(bf16[128,16,128]{2,1,0:T(8,128)(2,1)S(1)} %fusion.36.src_ref), custom_call_target="tpu_custom_call" | custom-call | tf_op jit(solution)/shard_map/pallas_call | solution.py:53
  170.3 4.4 tile.33
  174.7 6.6 %copy.30 = f32[6144,256]{0,1:T(8,128)} copy(f32[6144,256]{1,0:T(8,128)} %bitcast.171) | data formatting | bytes 12582912 | tf_op jit(solution)/shard_map/tile | solution.py:178
  181.3 24.9 %gather_fusion = bf16[6144,256]{1,0:T(8,128)(2,1)} fusion(bf16[1024,256]{1,0:T(8,128)(2,1)S(1)} %bitcast.165, s32[6144]{0:T(1024)S(1)} %broadcast_clamp_fusion), kind=kCustom, calls=%fused_computation.5 | custom fusion | bytes 6316032 | tf_op jit(solution)/shard_map/jit(_take)/gather | solution.py:116
  206.2 4.8 broadcast_select_fusion
  211.3 4.6 multiply_convert_fusion.1
  219.9 2.7 multiply_reduce_fusion
  222.6 3.4 multiply_convert_fusion
  226.1 4.7 convolution_bitcast_fusion
  230.8 5.2 fusion.77
  236.1 2.6 fusion.19
  238.7 6.4 %fusion.17 = f32[6144,512]{1,0:T(8,128)} fusion(bf16[6144,256]{1,0:T(8,128)(2,1)S(1)} %get-tuple-element.43, bf16[2,512,256]{2,1,0:T(8,128)(2,1)S(1)} %copy-done.23), kind=kOutput, calls=%fused_computation.56 | convolution fusion | flops 1610612736 | bytes 15990784 | tf_op jit(solution)/shard_map/dot_general | solution.py:107
  246.3 35.1 %scatter_custom_fusion.2 = f32[1024,256]{1,0:T(8,128)} fusion(s32[6144]{0:T(1024)S(1)} %bitcast.181, f32[6144,512]{1,0:T(8,128)} %fusion.17, f32[]{:T(128)} %constant.27.clone.1), kind=kCustom, calls=%fused_computation.15 | custom fusion | flops 1572864 | bytes 7340544 | tf_op jit(solution)/shard_map/scatter-add | solution.py:162
  282.8 15.9 %shard_map.184 = bf16[128,16,128]{2,1,0:T(8,128)(2,1)S(1)} custom-call(bf16[128,16,128]{2,1,0:T(8,128)(2,1)S(1)} %convert_bitcast_fusion.1.src_ref), custom_call_target="tpu_custom_call" | custom-call | tf_op jit(solution)/shard_map/pallas_call | solution.py:53
  298.7 9.1 %scatter_custom_fusion.3 = f32[1536,256]{1,0:T(8,128)} fusion(f32[1536,256]{1,0:T(8,128)} %convert_element_type.94, s32[1024]{0:T(1024)S(1)} %reshape.359, bf16[128,16,128]{2,1,0:T(8,128)(2,1)S(1)} %shard_map.184, f32[]{:T(128)} %constant.27.clone.1, pred[1024]{0:T(1024)(128)(4,1)S(1)} %ge.31), kind=kCustom, calls=%fused_computation.68 | custom fusion | flops 786432 | bytes 2098688 | tf_op jit(solution)/shard_map/scatter-add | solution.py:159
  309.3 4.3 gather_fusion.4
  314.0 16.0 %shard_map.185 = bf16[128,16,128]{2,1,0:T(8,128)(2,1)S(1)} custom-call(bf16[128,16,128]{2,1,0:T(8,128)(2,1)S(1)} %fusion.35.src_ref), custom_call_target="tpu_custom_call" | custom-call | tf_op jit(solution)/shard_map/pallas_call | solution.py:53
  330.0 17.0 %gather_fusion.5 = bf16[4096,256]{1,0:T(8,128)(2,1)} fusion(bf16[1024,256]{1,0:T(8,128)(2,1)S(1)} %bitcast.167, s32[4096]{0:T(1024)S(1)} %fusion.66), kind=kCustom, calls=%fused_computation.4.clone | custom fusion | bytes 4210688 | tf_op jit(solution)/shard_map/jit(_take)/gather | solution.py:186
  347.1 4.1 copy.31
  351.2 5.3 %fusion.11 = (f32[256]{0:T(256)S(1)}, f32[4096]{0:T(1024)S(1)}, f32[4096]{0:T(1024)S(1)}, f32[256]{0:T(256)S(1)}) fusion(f32[4096,256]{0,1:T(8,128)} %copy-done, f32[4096]{0:T(1024)S(1)} %add_rsqrt_fusion.1, f32[4096]{0:T(1024)S(1)} %broadcast_multiply_fusion.5, bf16[4096,256]{0,1:T(8,128)(2,1)} %copy.31, pred[4096]{0:T(1024)(128)(4,1)S(1)} %compare_and_fusion.1, ...), kind=kLoop, calls=%fused_computation.39 | loop fusion | flops 11525632 | bytes 6364160 | tf_op jit(solution)/shard_map/reduce_sum | solution.py:85
  360.4 2.0 fusion.78
  366.8 6.1 %fusion.30 = f32[4096,512]{1,0:T(8,128)} fusion(bf16[4096,256]{1,0:T(8,128)(2,1)} %copy-done.11, bf16[2,512,256]{2,1,0:T(8,128)(2,1)S(1)} %copy-done.24), kind=kOutput, calls=%fused_computation.74 | convolution fusion | flops 1073741824 | bytes 10747904 | tf_op jit(solution)/shard_map/dot_general | solution.py:107
  372.9 65.1 %all-reduce = (f32[2,256]{1,0:T(2,128)S(1)}, f32[2,256]{1,0:T(2,128)S(1)}, f32[2,256]{1,0:T(2,128)S(1)}) all-reduce(f32[2,256]{1,0:T(2,128)S(1)} %pad_maximum_fusion.14, f32[2,256]{1,0:T(2,128)S(1)} %get-tuple-element.48, f32[2,256]{1,0:T(2,128)S(1)} %get-tuple-element.49), channel_id=1, replica_groups=mesh['slab'=4,'brick'=32] {'slab','brick'}, use_global_device_ids=true, to_apply=%region_20.23 | all-reduce | flops 1536 | bytes 12288 | tf_op jit(solution)/shard_map/psum | solution.py:197
  437.9 23.4 %scatter_custom_fusion.4 = f32[1024,256]{1,0:T(8,128)S(1)} fusion(s32[4096]{0:T(1024)} %bitcast.190, f32[4096,512]{1,0:T(8,128)} %fusion.30, f32[]{:T(128)} %constant.27.clone.1), kind=kCustom, calls=%fused_computation.40 | custom fusion | flops 1048576 | bytes 5243392 | tf_op jit(solution)/shard_map/scatter-add | solution.py:162
  462.6 6.5 %slice.113 = f32[6144,256]{1,0:T(8,128)} slice(f32[6144,512]{1,0:T(8,128)} %fusion.17), slice={[0:6144], [0:256]} | slice | bytes 12582912 | tf_op jit(solution)/shard_map/slice | solution.py:193
  470.0 2.4 slice.115
  472.5 4.8 reduce_sum.150
  477.3 15.5 %shard_map.186 = bf16[128,16,128]{2,1,0:T(8,128)(2,1)S(1)} custom-call(bf16[128,16,128]{2,1,0:T(8,128)(2,1)S(1)} %convert_bitcast_fusion.src_ref), custom_call_target="tpu_custom_call" | custom-call | tf_op jit(solution)/shard_map/pallas_call | solution.py:53
  492.8 9.2 %scatter_custom_fusion.5 = f32[1536,256]{1,0:T(8,128)} fusion(f32[1536,256]{1,0:T(8,128)} %scatter_custom_fusion.3, s32[1024]{0:T(1024)S(1)} %reshape.359, bf16[128,16,128]{2,1,0:T(8,128)(2,1)S(1)} %shard_map.186, f32[]{:T(128)} %constant.27.clone.1, pred[1024]{0:T(1024)(128)(4,1)S(1)} %ge.31), kind=kCustom, calls=%fused_computation.65 | custom fusion | flops 786432 | bytes 2098688 | tf_op jit(solution)/shard_map/scatter-add | solution.py:159
  502.0 4.0 reduce_sum.153
  506.6 3.9 add_add_fusion
  510.5 3.5 all-reduce.4.cloned.1.call-done
  (148 shorter events, 38.7 us)
Async XLA Ops:
  7.2 34.0 %copy-start.3 = (bf16[1536,256]{1,0:T(8,128)(2,1)S(1)}, bf16[1536,256]{1,0:T(8,128)(2,1)}, u32[]{:S(2)}) copy-start(bf16[1536,256]{1,0:T(8,128)(2,1)} %param.18) | copy-start | bytes 2359300
  7.2 506.9 %all-reduce.4.cloned.1.call-start = ((), (), s32[]{:S(2)}) async-start(), calls=%async_computation | async-start | bytes 3145728 | tf_op jit(solution)/shard_map/psum | solution.py:197
  34.1 11.3 %copy-start.33 = (pred[1024]{0:T(1024)(128)(4,1)}, pred[1024]{0:T(1024)(128)(4,1)S(1)}, u32[]{:S(2)}) copy-start(pred[1024]{0:T(1024)(128)(4,1)S(1)} %compare_and_fusion.2) | copy-start | bytes 3076
  36.2 26.3 %copy-start.30 = (f32[1,256]{1,0:T(1,128)}, f32[1,256]{1,0:T(1,128)S(1)}, u32[]{:S(2)}) copy-start(f32[1,256]{1,0:T(1,128)S(1)} %get-tuple-element.30) | copy-start | bytes 3076
  36.2 51.4 %copy-start.35 = (f32[1,256]{1,0:T(1,128)}, f32[1,256]{1,0:T(1,128)S(1)}, u32[]{:S(2)}) copy-start(f32[1,256]{1,0:T(1,128)S(1)} %get-tuple-element.31) | copy-start | bytes 3076
  37.0 60.4 %copy-start.32 = (s32[4096,1]{0,1:T(1,128)}, s32[4096,1]{0,1:T(1,128)S(1)}, u32[]{:S(2)}) copy-start(s32[4096,1]{0,1:T(1,128)S(1)} %compare_select_fusion.1) | copy-start | bytes 49156
  80.5 2.1 copy-start.9
  80.5 2.2 copy-start.22
  82.5 3.3 copy-start.17
  82.7 3.1 copy-start.19
  82.7 3.1 copy-start.26
  85.8 1.3 copy-start.5
  87.1 1.9 copy-start
  87.1 1.9 slice-start.2
  206.2 4.8 copy-start.10
  206.2 5.0 copy-start.23
  206.2 5.1 copy-start.37
  211.0 4.9 copy-start.12
  211.2 4.7 copy-start.14
  211.3 4.6 copy-start.27
  215.9 1.8 copy-start.8
  215.9 3.3 slice-start
  215.9 4.0 slice-start.1
  217.6 2.2 copy-start.31
  226.1 4.7 copy-start.16
  230.8 5.3 %copy-start.13 = (bf16[6144,256]{1,0:T(8,128)(2,1)S(1)}, bf16[6144,256]{1,0:T(8,128)(2,1)}, u32[]{:S(2)}) copy-start(bf16[6144,256]{1,0:T(8,128)(2,1)} %copy-done.12) | copy-start | bytes 9437188
  230.8 5.3 %copy-start.15 = (bf16[3,2048,256]{2,1,0:T(8,128)(2,1)S(1)}, bf16[3,2048,256]{2,1,0:T(8,128)(2,1)}, u32[]{:S(2)}) copy-start(bf16[3,2048,256]{2,1,0:T(8,128)(2,1)} %copy-done.14) | copy-start | bytes 9437188
  238.7 6.4 %copy-start.21 = (bf16[1536,256]{1,0:T(8,128)(2,1)S(1)}, bf16[1536,256]{1,0:T(8,128)(2,1)}, u32[]{:S(2)}) copy-start(bf16[1536,256]{1,0:T(8,128)(2,1)} %param.20) | copy-start | bytes 2359300
  298.7 15.0 %copy-start.34 = (pred[1024]{0:T(1024)(128)(4,1)S(1)}, pred[1024]{0:T(1024)(128)(4,1)}, u32[]{:S(2)}) copy-start(pred[1024]{0:T(1024)(128)(4,1)} %copy-done.33) | copy-start | bytes 3076
  347.1 4.1 copy-start.36
  351.1 5.4 %copy-start.1 = (f32[4096,256]{0,1:T(8,128)S(1)}, f32[4096,256]{0,1:T(8,128)}, u32[]{:S(2)}) copy-start(f32[4096,256]{0,1:T(8,128)} %copy-done) | copy-start | bytes 12582916
  351.1 5.4 %copy-start.4 = (bf16[4096,256]{0,1:T(8,128)(2,1)S(1)}, bf16[4096,256]{0,1:T(8,128)(2,1)}, u32[]{:S(2)}) copy-start(bf16[4096,256]{0,1:T(8,128)(2,1)} %copy.31) | copy-start | bytes 6291460
  356.5 1.6 copy-start.6
  358.1 0.9 copy-start.28
  358.1 2.3 copy-start.38
  360.4 2.0 copy-start.18
  360.4 2.2 copy-start.20
  362.4 1.6 copy-start.11
  362.6 1.4 copy-start.25
  362.6 2.5 copy-start.29
  364.1 2.7 copy-start.24
  462.6 7.4 %copy-start.2 = (f32[4096,512]{1,0:T(8,128)S(1)}, f32[4096,512]{1,0:T(8,128)}, u32[]{:S(2)}) copy-start(f32[4096,512]{1,0:T(8,128)} %fusion.30) | copy-start | bytes 25165828
  492.7 13.9 %copy-start.7 = (bf16[2048,256]{1,0:T(8,128)(2,1)S(1)}, bf16[2048,256]{1,0:T(8,128)(2,1)}, u32[]{:S(2)}) copy-start(bf16[2048,256]{1,0:T(8,128)(2,1)} %param.19) | copy-start | bytes 3145732
Sparse Core Ops, SparseCore 0:
  366.1 147.9 all-reduce.3

commit v2 on v0

v2 whole, which is shorter than its diff:
```python
import functools
import math

import jax
import jax.numpy as jnp
from jax import lax
from jax.experimental import pallas as pl
from jax.experimental.pallas import tpu as pltpu
from jax.sharding import PartitionSpec as P

EPS = 1e-05
LANES = 128
BF16 = jnp.bfloat16
F32 = jnp.float32
ENC, DEC = 0, 1
PART_WIRE = (BF16, F32)


def dot(a, b):
    return jnp.dot(a, b, preferred_element_type=F32)


def dot_tn(a, b):
    return lax.dot_general(a, b, (((0,), (0,)), ((), ())), preferred_element_type=F32)


def dot_nt(a, b):
    return lax.dot_general(a, b, (((1,), (1,)), ((), ())), preferred_element_type=F32)


def to_blocks(rows):
    parts = rows.reshape(rows.shape[0] // 8, 8, 2 * LANES)
    return jnp.concatenate([parts[:, :, :LANES], parts[:, :, LANES:]], axis=1).astype(BF16)


def from_blocks(blocks):
    parts = blocks.astype(F32)
    parts = jnp.concatenate([parts[:, :8], parts[:, 8:]], axis=2)
    return parts.reshape(blocks.shape[0] * 8, 2 * LANES)


def one_hot(match):
    return jnp.where(match, jnp.ones((), BF16), jnp.zeros((), BF16))


def fold(rows):
    return jnp.sum(rows.reshape(rows.shape[0] // 8, 8, rows.shape[1]), axis=0)


class Sizes:
    def __init__(self, slabs, bricks, cells, mesh_rows, enc_k, dec_k):
        self.slabs, self.bricks = slabs, bricks
        self.peers = slabs * bricks
        self.cells, self.mesh_rows = cells, mesh_rows
        self.fanout = (enc_k, dec_k)
        self.slots = 8 * self.peers
        self.tile = min(1024, cells)
        self.chunk = min(512, self.slots)
        self.own_rows = math.gcd(512, mesh_rows)
        self.per_owner = -(-97 // self.peers)
        self.owners = -(-97 // self.per_owner)


def kernel(
    sz,
    grid_ref, lat_ref, cot_ref, mesh_cot_ref, w1_ref, w2_ref, bias_ref, gain_ref, shift_ref,
    ask_ref, enc_row_ref, dec_row_ref, enc_pack_ref, dec_pack_ref,
    grid_out, mesh_out, w1_out, w2_out, bias_out, gain_out, shift_out,
    asked, ask_col, ask_row, enc_col, dec_col, base, table, stage, landed,
    pre, xm, outer_low, hidden, deriv, normed, invstd, edge_low,
    cell_sum, mid, mid_grad, slot_sum, parts, part_vec, rs_src_enc, rs_src_dec, rs_land_enc, rs_land_dec,
    ag_src_enc, ag_src_dec, ag_land_enc, ag_land_dec,
    send_sem, recv_sem, rs_send, rs_recv, ag_send, ag_recv,
):
    peers, slots, tile, chunk = sz.peers, sz.slots, sz.tile, sz.chunk
    me = lax.axis_index("slab") * sz.bricks + lax.axis_index("brick")
    row_refs, pack_refs, cols = (enc_row_ref, dec_row_ref), (enc_pack_ref, dec_pack_ref), (enc_col, dec_col)

    rs_src, rs_land = (rs_src_enc, rs_src_dec), (rs_land_enc, rs_land_dec)
    ag_src, ag_land = (ag_src_enc, ag_src_dec), (ag_land_enc, ag_land_dec)

    def place(peer):
        return (peer // sz.bricks, lax.rem(peer, sz.bricks))

    def loop(count, body):
        def step(index, carry):
            body(index)
            return carry

        lax.fori_loop(0, count, step, 0)

    def rows_of(index, size):
        return pl.ds(pl.multiple_of(index * size, size), size)

    barrier = pltpu.get_barrier_semaphore()

    def greet(step, carry):
        pl.semaphore_signal(
            barrier, inc=1, device_id=place(lax.rem(me + step, peers)),
            device_id_type=pl.DeviceIdType.MESH,
        )
        return carry

    lax.fori_loop(1, peers, greet, 0)
    pl.semaphore_wait(barrier, peers - 1)

    def ask(step, carry):
        peer = lax.rem(me + step, peers)
        pltpu.make_async_remote_copy(
            src_ref=ask_ref.at[peer], dst_ref=asked.at[peers - step],
            send_sem=send_sem.at[0], recv_sem=recv_sem.at[0],
            device_id=place(peer), device_id_type=pl.DeviceIdType.MESH,
        ).start()
        return carry

    lax.fori_loop(1, peers, ask, 0)
    asked[0] = ask_ref[me]

    def send(phase, start, stop):
        def one(step, carry):
            pltpu.make_async_remote_copy(
                src_ref=stage.at[phase - 1, step], dst_ref=landed.at[phase - 1, peers - step],
                send_sem=send_sem.at[phase], recv_sem=recv_sem.at[phase],
                device_id=place(lax.rem(me + step, peers)), device_id_type=pl.DeviceIdType.MESH,
            ).start()
            return carry

        lax.fori_loop(max(start, 1), stop, one, 0)
        if start == 0:
            landed[phase - 1, 0] = stage[phase - 1, 0]

    def wait(sem, ref, count):
        span = ref.at[pl.ds(0, count)]
        pltpu.make_async_copy(span, span, sem).wait()

    def wait_rows(phase):
        wait(recv_sem.at[phase], landed.at[phase - 1], peers - 1)

    for layer in (ENC, DEC):
        def cell_part(index, layer=layer):
            span = rows_of(index, tile)
            base[layer, span] = dot(grid_ref[span], w1_ref[layer, :256]) + bias_ref[layer:layer + 1]

        loop(sz.cells // tile, cell_part)

        def column(index, layer=layer):
            row = pack_refs[layer][pl.ds(index, 1), :].astype(F32)
            square = jnp.transpose(jnp.broadcast_to(row, (LANES, LANES)))
            cols[layer][rows_of(index, LANES)] = square.astype(jnp.int32)

        loop(sz.fanout[layer] * sz.cells // LANES, column)

    wait(recv_sem.at[0], asked, peers - 1)
    wide = asked[...].astype(F32)
    wide = jnp.broadcast_to(wide, (peers, 8, LANES))
    lane = lax.broadcasted_iota(jnp.int32, (peers, 8, LANES), 2)
    sub = lax.broadcasted_iota(jnp.int32, (peers, 8, LANES), 1)
    picked = jnp.sum(jnp.where(lane == sub, wide, 0.0), axis=2, keepdims=True)
    picked = jnp.broadcast_to(picked, (peers, 8, LANES)).reshape(slots, LANES)
    ask_col[...] = picked.astype(jnp.int32)
    for index in range(slots // LANES):
        square = jnp.transpose(picked[index * LANES:(index + 1) * LANES])
        ask_row[:, index * LANES:(index + 1) * LANES] = square[:8].astype(jnp.int32)

    def serve(phase, source):
        for start in range(0, slots, chunk):
            column = ask_col[start:start + chunk]
            lanes = lax.broadcasted_iota(jnp.int32, (chunk, LANES), 1)
            chosen = jnp.concatenate(
                [one_hot(column == lanes + first) for first in range(0, sz.mesh_rows, LANES)], axis=1
            )[:, :sz.mesh_rows]
            stage[phase - 1, start // 8:(start + chunk) // 8] = to_blocks(dot(chosen, source[...]))
            send(phase, start // 8, (start + chunk) // 8)

    def fetch(phase):
        wait_rows(phase)
        table[...] = from_blocks(landed[phase - 1]).astype(BF16)

    def returned(phase, target, span):
        row = jnp.broadcast_to(ask_row[0:1], (sz.own_rows, slots))
        sub = lax.broadcasted_iota(jnp.int32, (sz.own_rows, slots), 0) + target
        return dot(one_hot(row == sub), table[...])

    def gather(layer, index):
        column = cols[layer][rows_of(index, tile)]
        lanes = lax.broadcasted_iota(jnp.int32, (tile, LANES), 1)
        chosen = jnp.concatenate(
            [one_hot(column == lanes + first) for first in range(0, slots, LANES)], axis=1
        )
        return dot(chosen, table[...])

    def slot_sums(layer, start):
        slot_sum[...] = jnp.zeros_like(slot_sum)

        def add(index):
            row = jnp.broadcast_to(row_refs[layer][pl.ds(index, 1), :], (chunk, tile))
            sub = lax.broadcasted_iota(jnp.int32, (chunk, tile), 0) + start
            slot_sum[...] += dot(one_hot(row == sub), edge_low[rows_of(index, tile)])

        loop(sz.fanout[layer] * sz.cells // tile, add)

    def cells_of(layer, index):
        return lax.rem(index, sz.cells // tile) * tile

    fine = min(128, tile)

    def first_half(layer, index, hid_ref, hid_base):
        xm[...] = gather(layer, index).astype(BF16)
        pre[...] = dot(xm[...], w1_ref[layer, 256:])
        cell = cells_of(layer, index)

        def act(part):
            span = rows_of(part, fine)
            x = pre[span] + base[layer, pl.ds(pl.multiple_of(cell + part * fine, fine), fine)]
            gate = 0.5 * jnp.tanh(0.5 * x) + 0.5
            value = x * gate
            hid_ref[pl.ds(pl.multiple_of(hid_base + part * fine, fine), fine)] = value.astype(BF16)
            deriv[pl.ds(pl.multiple_of(hid_base + part * fine, fine), fine)] = gate + value * (1.0 - gate)

        loop(tile // fine, act)
        pre[...] = dot(hid_ref[pl.ds(pl.multiple_of(hid_base, tile), tile)], w2_ref[layer])

    def normalise(x):
        center = x - jnp.mean(x, axis=-1, keepdims=True)
        inv = lax.rsqrt(jnp.mean(center * center, axis=-1, keepdims=True) + EPS)
        return center * inv, inv

    def outer_back(layer, unit, inv, cot):
        grad = cot * gain_ref[layer:layer + 1]
        weighed = cot * unit
        out = inv * (
            grad
            - jnp.mean(grad, axis=-1, keepdims=True)
            - unit * jnp.mean(grad * unit, axis=-1, keepdims=True)
        )
        return out, fold(weighed), fold(cot)

    def accumulate(slot, value):
        part_vec[slot] += value

    def second_back(layer, index, hid_ref, hid_base):
        parts[512:768] += dot_tn(hid_ref[pl.ds(pl.multiple_of(hid_base, tile), tile)], outer_low[...])
        pre[...] = dot_nt(outer_low[...], w2_ref[layer])
        cell = cells_of(layer, index)

        def act(part):
            grad = pre[rows_of(part, fine)] * deriv[pl.ds(pl.multiple_of(hid_base + part * fine, fine), fine)]
            accumulate(0, fold(grad))
            low = grad.astype(BF16)
            edge_low[pl.ds(pl.multiple_of(index * tile + part * fine, fine), fine)] = low
            span = pl.ds(pl.multiple_of(cell + part * fine, fine), fine)
            cell_sum[span] += low.astype(F32)

        loop(tile // fine, act)

    def send_slot_grads(layer, phase):
        for start in range(0, slots, chunk):
            slot_sum_chunk(layer, phase, start)

    def slot_sum_chunk(layer, phase, start):
        slot_sums(layer, start)
        total = slot_sum[...]
        high = total.astype(BF16)
        low = (total - high.astype(F32)).astype(BF16)
        weight = w1_ref[layer, 256:]
        stage[phase - 1, start // 8:(start + chunk) // 8] = to_blocks(dot_nt(high, weight) + dot_nt(low, weight))
        send(phase, start // 8, (start + chunk) // 8)
        rows = table[start:start + chunk]
        parts[256:512] += dot_tn(rows, high) + dot_tn(rows, low)

    def cell_back(layer):
        def one(index):
            span = rows_of(index, tile)
            total = cell_sum[span]
            high = total.astype(BF16)
            low = (total - high.astype(F32)).astype(BF16)
            weight, rows = w1_ref[layer, :256], grid_ref[span]
            grid_out[span] += dot_nt(high, weight) + dot_nt(low, weight)
            parts[0:256] += dot_tn(rows, high) + dot_tn(rows, low)

        loop(sz.cells // tile, one)

    def owner_of(layer, block):
        return block if layer == ENC else peers - 1 - block

    def clear_parts():
        parts[...] = jnp.zeros_like(parts)
        part_vec[...] = jnp.zeros_like(part_vec)
        cell_sum[...] = jnp.zeros_like(cell_sum)

    def send_parts(layer):
        flat = jnp.concatenate(
            [
                parts[256 * which:256 * which + 256, LANES * side:LANES * side + LANES].reshape(16, 16, LANES)
                for which in range(3) for side in range(2)
            ]
        ).astype(PART_WIRE[layer])
        per = sz.per_owner
        pieces = [jnp.sum(part_vec[which], axis=0, keepdims=True) for which in range(3)]
        halves = [piece[:, LANES * side:LANES * side + LANES] for piece in pieces for side in range(2)]
        last = jnp.concatenate(halves + [jnp.zeros((10, LANES), F32)], axis=0).astype(PART_WIRE[layer])
        for block in range(96):
            rs_src[layer][block // per, (block % per) * 16:(block % per) * 16 + 16] = flat[block]
        rs_src[layer][96 // per, (96 % per) * 16:(96 % per) * 16 + 16] = last
        for block in range(97, sz.owners * per):
            rs_src[layer][block // per, (block % per) * 16:(block % per) * 16 + 16] = jnp.zeros((16, LANES), PART_WIRE[layer])

        def one(block):
            target = owner_of(layer, block)

            @pl.when(target != me)
            def _():
                pltpu.make_async_remote_copy(
                    src_ref=rs_src[layer].at[block], dst_ref=rs_land[layer].at[me],
                    send_sem=rs_send.at[layer], recv_sem=rs_recv.at[layer],
                    device_id=place(target), device_id_type=pl.DeviceIdType.MESH,
                ).start()

        loop(sz.owners, one)

    def sum_parts(layer):
        mine = owner_of(layer, me)

        @pl.when(mine < sz.owners)
        def _():
            rs_land[layer][me] = rs_src[layer][mine]
            wait(rs_recv.at[layer], rs_land[layer], peers - 1)
            scale = 1.0 / math.sqrt(sz.fanout[layer] * sz.cells * peers)
            total = (jnp.sum(rs_land[layer][...].astype(F32), axis=0) * scale).astype(PART_WIRE[layer])
            ag_src[layer][...] = total
            ag_land[layer][mine] = total

            def one(step, carry):
                pltpu.make_async_remote_copy(
                    src_ref=ag_src[layer], dst_ref=ag_land[layer].at[mine],
                    send_sem=ag_send.at[layer], recv_sem=ag_recv.at[layer],
                    device_id=place(lax.rem(me + step, peers)), device_id_type=pl.DeviceIdType.MESH,
                ).start()
                return carry

            lax.fori_loop(1, peers, one, 0)

    def finish_parts(layer):
        mine = owner_of(layer, me)
        @pl.when(mine >= sz.owners)
        def _():
            wait(ag_recv.at[layer], ag_land[layer], sz.owners)
            wait(rs_send.at[layer], rs_src[layer], sz.owners)

        @pl.when(mine < sz.owners)
        def _():
            wait(ag_recv.at[layer], ag_land[layer], sz.owners - 1)
            wait(rs_send.at[layer], rs_src[layer], sz.owners - 1)
            wait(ag_send.at[layer], rs_land[layer], peers - 1)

        flat = ag_land[layer][...].astype(F32).reshape(sz.owners * sz.per_owner, 16, LANES)
        matrix = [
            jnp.concatenate(
                [flat[32 * which + 16 * side:32 * which + 16 * side + 16].reshape(256, LANES) for side in range(2)],
                axis=1,
            )
            for which in range(3)
        ]
        w1_out[layer, :256] = matrix[0]
        w1_out[layer, 256:] = matrix[1]
        w2_out[layer] = matrix[2]
        last = flat[96]
        for which, out in enumerate((bias_out, gain_out, shift_out)):
            out[layer:layer + 1] = jnp.concatenate([last[2 * which:2 * which + 1], last[2 * which + 1:2 * which + 2]], axis=1)

    serve(1, lat_ref)
    clear_parts()
    grid_out[...] = cot_ref[...].astype(F32)
    fetch(1)
    broad = min(256, tile)

    def encode(index):
        first_half(ENC, index, hidden, index * tile)

        def act(part):
            span = pl.ds(pl.multiple_of(index * tile + part * broad, broad), broad)
            unit, inv = normalise(pre[rows_of(part, broad)])
            normed[span] = unit
            invstd[span] = inv
            edge_low[span] = (unit * gain_ref[ENC:ENC + 1] + shift_ref[ENC:ENC + 1]).astype(BF16)

        loop(tile // broad, act)

    loop(sz.fanout[ENC] * sz.cells // tile, encode)
    for start in range(0, slots, chunk):
        slot_sums(ENC, start)
        stage[1, start // 8:(start + chunk) // 8] = to_blocks(slot_sum[...])
        send(2, start // 8, (start + chunk) // 8)

    fetch(2)

    def make_mid(index):
        span = rows_of(index, sz.own_rows)
        mid[span] = (lat_ref[span].astype(F32) + returned(2, index * sz.own_rows, span)).astype(BF16)

    loop(sz.mesh_rows // sz.own_rows, make_mid)
    serve(3, mid)
    fetch(3)

    def decode(index):
        behind = sz.fanout[ENC] * sz.cells
        first_half(DEC, index, hidden, behind)
        cell = cells_of(DEC, index)

        def act(part):
            unit, inv = normalise(pre[rows_of(part, broad)])
            cot = cot_ref[pl.ds(pl.multiple_of(cell + part * broad, broad), broad)].astype(F32)
            out, gain, shift = outer_back(DEC, unit, inv, cot)
            accumulate(1, gain)
            accumulate(2, shift)
            outer_low[rows_of(part, broad)] = out.astype(BF16)

        loop(tile // broad, act)
        second_back(DEC, index, hidden, behind)

    loop(sz.fanout[DEC] * sz.cells // tile, decode)
    send_slot_grads(DEC, 4)
    cell_back(DEC)
    send_parts(DEC)

    fetch(4)

    def make_mid_grad(index):
        span = rows_of(index, sz.own_rows)
        total = mesh_cot_ref[span].astype(F32) + returned(4, index * sz.own_rows, span)
        mid_grad[span] = total
        mid[span] = total.astype(BF16)

    loop(sz.mesh_rows // sz.own_rows, make_mid_grad)
    serve(5, mid)
    clear_parts()
    sum_parts(DEC)
    fetch(5)

    def encode_back(index):
        pre[...] = gather(ENC, index)

        def act(part):
            span = pl.ds(pl.multiple_of(index * tile + part * broad, broad), broad)
            out, gain, shift = outer_back(ENC, normed[span], invstd[span], pre[rows_of(part, broad)])
            accumulate(1, gain)
            accumulate(2, shift)
            outer_low[rows_of(part, broad)] = out.astype(BF16)

        loop(tile // broad, act)
        second_back(ENC, index, hidden, index * tile)

    loop(sz.fanout[ENC] * sz.cells // tile, encode_back)
    table[...] = from_blocks(landed[0]).astype(BF16)
    send_slot_grads(ENC, 6)
    cell_back(ENC)
    send_parts(ENC)

    fetch(6)

    def make_mesh_out(index):
        span = rows_of(index, sz.own_rows)
        mesh_out[span] = mid_grad[span] + returned(6, index * sz.own_rows, span)

    loop(sz.mesh_rows // sz.own_rows, make_mesh_out)
    sum_parts(ENC)
    finish_parts(DEC)
    finish_parts(ENC)
    wait(send_sem.at[0], asked, peers - 1)
    for phase in range(1, 7):
        wait(send_sem.at[phase], landed.at[phase - 1], peers - 1)


def per_device(
    grid_latent, mesh_node_latents, grid_cot, mesh_cotangent, w_first, w_second, biases, ln_gain,
    ln_shift, requests, counts, enc_slots, dec_slots,
):
    slabs, bricks = lax.axis_size("slab"), lax.axis_size("brick")
    cells, features = grid_latent.shape
    mesh_rows = mesh_node_latents.shape[0]
    sz = Sizes(slabs, bricks, cells, mesh_rows, enc_slots.shape[0], dec_slots.shape[0])
    peers, slots, tile = sz.peers, sz.slots, sz.tile
    me = lax.axis_index("slab") * bricks + lax.axis_index("brick")
    positions = lax.broadcasted_iota(jnp.int32, (peers, 8), 1)
    asking = jnp.where(positions < counts.reshape(peers, 1), requests, -1)
    asking = jnp.pad(asking, ((0, 0), (0, LANES - 8))).reshape(peers, 1, LANES)
    enc_turned = lax.rem(enc_slots - 8 * me + slots, slots)
    dec_turned = lax.rem(dec_slots - 8 * me + slots, slots)
    enc_edges, dec_edges = sz.fanout[ENC] * cells, sz.fanout[DEC] * cells
    vmem = pl.BlockSpec(memory_space=pltpu.VMEM)
    outs = [
        jax.ShapeDtypeStruct(shape, F32)
        for shape in (
            (cells, features), (mesh_rows, features), (2, 2 * features, features),
            (2, features, features), (2, features), (2, features), (2, features),
        )
    ]
    dma = pltpu.SemaphoreType.DMA
    per = sz.per_owner
    scratch = [
        pltpu.VMEM((peers, 1, LANES), jnp.int32),
        pltpu.VMEM((slots, LANES), jnp.int32),
        pltpu.VMEM((8, slots), jnp.int32),
        pltpu.VMEM((enc_edges, LANES), jnp.int32),
        pltpu.VMEM((dec_edges, LANES), jnp.int32),
        pltpu.VMEM((2, cells, features), F32),
        pltpu.VMEM((slots, features), BF16),
        pltpu.VMEM((6, peers, 16, LANES), BF16),
        pltpu.VMEM((6, peers, 16, LANES), BF16),
        pltpu.VMEM((tile, features), F32),
        pltpu.VMEM((tile, features), BF16),
        pltpu.VMEM((tile, features), BF16),
        pltpu.VMEM((enc_edges + tile, features), BF16),
        pltpu.VMEM((enc_edges + tile, features), F32),
        pltpu.VMEM((enc_edges, features), F32),
        pltpu.VMEM((enc_edges, 1), F32),
        pltpu.VMEM((dec_edges, features), BF16),
        pltpu.VMEM((cells, features), F32),
        pltpu.VMEM((mesh_rows, features), BF16),
        pltpu.VMEM((mesh_rows, features), F32),
        pltpu.VMEM((sz.chunk, features), F32),
        pltpu.VMEM((3 * features, features), F32),
        pltpu.VMEM((3, 8, features), F32),
        *[pltpu.VMEM((sz.owners, per * 16, LANES), kind) for kind in PART_WIRE],
        *[pltpu.VMEM((peers, per * 16, LANES), kind) for kind in PART_WIRE],
        *[pltpu.VMEM((per * 16, LANES), kind) for kind in PART_WIRE],
        *[pltpu.VMEM((sz.owners, per * 16, LANES), kind) for kind in PART_WIRE],
        dma((7,)), dma((7,)), dma((2,)), dma((2,)), dma((2,)), dma((2,)),
    ]
    return tuple(
        pl.pallas_call(
            functools.partial(kernel, sz),
            out_shape=outs,
            in_specs=[vmem] * 14,
            out_specs=[vmem] * 7,
            scratch_shapes=scratch,
            compiler_params=pltpu.CompilerParams(
                collective_id=1, has_side_effects=True, vmem_limit_bytes=62 << 20
            ),
        )(
            grid_latent, mesh_node_latents, grid_cot, mesh_cotangent, w_first, w_second,
            biases, ln_gain, ln_shift, asking,
            enc_turned.reshape(enc_edges // tile, tile), dec_turned.reshape(dec_edges // tile, tile),
            enc_turned.reshape(enc_edges // LANES, LANES), dec_turned.reshape(dec_edges // LANES, LANES),
        )
    )


def solution(mesh):
    split = P(("slab", "brick"), None)
    edges = P(None, ("slab", "brick"))
    return jax.shard_map(
        per_device,
        mesh=mesh,
        in_specs=(split, split, split, split, P(), P(), P(), P(), P(), split, split, edges, edges),
        out_specs=(split, split, P(), P(), P(), P(), P()),
        check_vma=False,
    )
```

time: 674 us -> 203 us (0.30)
  waiting for transfers between devices: 204 us -> 0 us
  Pallas kernels: 0 us -> 187 us
  other arithmetic: 171 us -> 2.25 us
  local copies, waits for them, and re-layouts: 119 us -> 12.4 us
  blocking collectives: 67.7 us -> 0 us
  starting transfers between devices: 48.5 us -> 0 us
  matrix products: 42.4 us -> 0 us
  between operations: 15 us -> 0.68 us
    pallas_call x0 -> x1, Pallas kernels: none -> 187 us  [per_device(): pl.pallas_call(functools.partial(kernel, sz), out_shape=outs, in_specs=[v...]
    psum x1 -> x0, waiting for transfers between devices: 148 us -> none  [per_device(): lax.psum((stacked[0], stacked[1], stacked[2], stacked[3], stacked[4]), ('...]
    scatter-add x6 -> x0, other arithmetic: 109 us -> none  [the longest x3 83.3 us: slot_sums(): jnp.zeros((slot_total, features), jnp.float32).at[slot_ids.reshape(-1)]]
    gather x7 -> x0, local copies, waits for them, and re-layouts: 75.3 us -> none  [the longest x2 42.1 us: local_inputs(): mesh_rows = jnp.take(gathered_rows, slot_ids.reshape(-1), axis=0)]
    psum x1 -> x0, blocking collectives: 67.7 us -> none  [per_device(): lax.psum((stacked[0], stacked[1], stacked[2], stacked[3], stacked[4]), ('...]
    all_to_all x8 -> x0, waiting for transfers between devices: 56.7 us -> none  [the longest x3 33.9 us: collect(): lax.all_to_all(blocks, ('slab', 'brick'), split_axis=0, concat_axis=0, ti...]
    all_to_all x8 -> x0, starting transfers between devices: 48.4 us -> none  [the longest x3 17.4 us: collect(): lax.all_to_all(blocks, ('slab', 'brick'), split_axis=0, concat_axis=0, ti...]
    dot_general x12 -> x0, matrix products: 42.4 us -> none  [the longest x2 10.9 us: edge_backward(): lax.dot_general(preact_low, first_layer, (((1,), (1,)), ((), ())), prefer...]
  transfers between devices with their start and end apart: 9 -> 0, of which waited for: 7 -> 0; matrix products, arithmetic and copies ran while one was open for 9% -> 0% of each run, Pallas kernels for 0% -> 0%
where the time goes in v2:
time: 203 us
  Pallas kernels  187 us (92%)
  local copies, waits for them, and re-layouts  12.4 us (6%)
  other arithmetic  2.25 us (1%)
    pallas_call x1, Pallas kernels, per_device(): pl.pallas_call(functools.partial(kernel, sz), out_shape=outs, in_specs=[v...  187 us
    unnamed x20, local copies, waits for them, and re-layouts  9.25 us

profile of v2, /device:TPU:1, one launch (start us, length us, event | category | flops | bytes accessed | tf_op | source)
XLA Modules:
  0.0 202.8 jit_solution(8370340874116250530)
XLA Ops:
  0.6 0.7 compare_select_fusion
  1.4 0.6 reshape.34.enc_pack_ref
  2.0 0.6 reshape.32.enc_row_ref
  2.6 0.8 negate_select_fusion
  3.4 0.6 reshape.35.dec_pack_ref
  4.0 0.6 reshape.33.dec_row_ref
  4.7 0.8 copy.20
  5.5 0.7 fusion
  6.2 0.6 pad.4
  6.8 187.4 %shard_map.180 = (f32[2048,256]{1,0:T(8,128)}, f32[1536,256]{1,0:T(8,128)}, f32[2,512,256]{2,1,0:T(8,128)}, f32[2,256,256]{2,1,0:T(8,128)}, f32[2,256]{1,0:T(2,1...) custom-call(bf16[2048,256]{1,0:T(8,128)(2,1)} %grid_ref.1, bf16[1536,256]{1,0:T(8,128)(2,1)} %lat_ref.1, ...), custom_call_target="tpu_custom_call" | custom-call | tf_op jit(solution)/shard_map/pallas_call | solution.py:531
  194.3 0.0 copy-start
  194.3 3.2 %copy.28 = f32[2048,256]{1,0:T(8,128)} copy(f32[2048,256]{1,0:T(8,128)} %get-tuple-element.14) | data formatting | bytes 4194304
  197.4 0.0 copy-done
  197.4 0.0 copy-start.1
  197.4 0.0 copy-start.2
  197.4 1.1 copy.29
  198.6 0.6 copy-done.1
  199.2 0.0 copy-start.5
  199.2 0.0 copy-start.4
  199.2 0.0 copy-start.3
  199.2 1.0 copy.30
  200.2 0.0 copy-done.2
  200.2 0.8 copy.31
  201.0 0.0 copy-done.5
  201.0 0.6 copy.32
  201.6 0.0 copy-done.4
  201.6 0.6 copy.33
  202.2 0.0 copy-done.3
  202.2 0.6 copy.34
Async XLA Ops:
  194.3 3.2 %copy-start = (f32[1536,256]{1,0:T(8,128)S(1)}, f32[1536,256]{1,0:T(8,128)}, u32[]{:S(2)}) copy-start(f32[1536,256]{1,0:T(8,128)} %get-tuple-element.15) | copy-start | bytes 4718596
  197.4 1.8 copy-start.1
  197.4 2.8 %copy-start.2 = (f32[2,256,256]{2,1,0:T(8,128)S(1)}, f32[2,256,256]{2,1,0:T(8,128)}, u32[]{:S(2)}) copy-start(f32[2,256,256]{2,1,0:T(8,128)} %get-tuple-element.17) | copy-start | bytes 1572868
  199.2 1.8 copy-start.5
  199.2 2.4 %copy-start.4 = (f32[2,256]{1,0:T(2,128)S(1)}, f32[2,256]{1,0:T(2,128)}, u32[]{:S(2)}) copy-start(f32[2,256]{1,0:T(2,128)} %get-tuple-element.19) | copy-start | bytes 6148
  199.2 2.9 %copy-start.3 = (f32[2,256]{1,0:T(2,128)S(1)}, f32[2,256]{1,0:T(2,128)}, u32[]{:S(2)}) copy-start(f32[2,256]{1,0:T(2,128)} %get-tuple-element.20) | copy-start | bytes 6148

commit v3 on v2

--- a/solution.py
+++ b/solution.py
@@ -57,32 +57,42 @@
         self.tile = min(1024, cells)
         self.chunk = min(512, self.slots)
         self.own_rows = math.gcd(512, mesh_rows)
-        self.per_owner = -(-97 // self.peers)
-        self.owners = -(-97 // self.per_owner)
+        self.near = bricks // 4 if bricks >= 16 else 4
+        self.far = self.peers // self.near
+        share = -(-97 // self.near)
+        self.piece = -(-share // self.far)
+        self.active = -(-share // self.piece)
 
 
 def kernel(
     sz,
     grid_ref, lat_ref, cot_ref, mesh_cot_ref, w1_ref, w2_ref, bias_ref, gain_ref, shift_ref,
-    ask_ref, enc_row_ref, dec_row_ref, enc_pack_ref, dec_pack_ref,
+    ask_ref, enc_row_ref, dec_row_ref,
     grid_out, mesh_out, w1_out, w2_out, bias_out, gain_out, shift_out,
-    asked, ask_col, ask_row, enc_col, dec_col, base, table, stage, landed,
+    asked, ask_col, ask_row, enc_row, dec_row, enc_col, dec_col, base, table, stage, landed,
     pre, xm, outer_low, hidden, deriv, normed, invstd, edge_low,
-    cell_sum, mid, mid_grad, slot_sum, parts, part_vec, rs_src_enc, rs_src_dec, rs_land_enc, rs_land_dec,
-    ag_src_enc, ag_src_dec, ag_land_enc, ag_land_dec,
-    send_sem, recv_sem, rs_send, rs_recv, ag_send, ag_recv,
+    cell_sum, mid, mid_grad, slot_sum, parts, part_vec,
+    near_src_enc, near_src_dec, near_land_enc, near_land_dec, far_src_enc, far_src_dec, far_land_enc, far_land_dec,
+    far_sum_enc, far_sum_dec, near_sum_enc, near_sum_dec, far_wide_enc, far_wide_dec,
+    send_sem, recv_sem, part_send, part_recv,
 ):
     peers, slots, tile, chunk = sz.peers, sz.slots, sz.tile, sz.chunk
     me = lax.axis_index("slab") * sz.bricks + lax.axis_index("brick")
-    row_refs, pack_refs, cols = (enc_row_ref, dec_row_ref), (enc_pack_ref, dec_pack_ref), (enc_col, dec_col)
-
-    rs_src, rs_land = (rs_src_enc, rs_src_dec), (rs_land_enc, rs_land_dec)
-    ag_src, ag_land = (ag_src_enc, ag_src_dec), (ag_land_enc, ag_land_dec)
+    row_refs, rows, cols = (enc_row_ref, dec_row_ref), (enc_row, dec_row), (enc_col, dec_col)
+
+    near_src, near_land = (near_src_enc, near_src_dec), (near_land_enc, near_land_dec)
+    far_src, far_land = (far_src_enc, far_src_dec), (far_land_enc, far_land_dec)
+    far_sum, near_sum = (far_sum_enc, far_sum_dec), (near_sum_enc, near_sum_dec)
+    far_wide = (far_wide_enc, far_wide_dec)
+    group, member = me // sz.near, lax.rem(me, sz.near)
 
     def place(peer):
         return (peer // sz.bricks, lax.rem(peer, sz.bricks))
 
     def loop(count, body):
+        if count == 1:
+            return body(0)
+
         def step(index, carry):
             body(index)
             return carry
@@ -90,7 +100,24 @@
         lax.fori_loop(0, count, step, 0)
 
     def rows_of(index, size):
+        if isinstance(index, int):
+            return pl.ds(index * size, size)
         return pl.ds(pl.multiple_of(index * size, size), size)
+
+    def local_work(layer):
+        def cell_part(index):
+            span = rows_of(index, tile)
+            base[layer, span] = dot(grid_ref[span], w1_ref[layer, :256]) + bias_ref[layer:layer + 1]
+
+        loop(sz.cells // tile, cell_part)
+        for which in range(sz.fanout[layer]):
+            turned = row_refs[layer][which:which + 1].astype(F32) - (8 * me).astype(F32)
+            turned = jnp.where(turned < 0.0, turned + slots, turned)
+            rows[layer][which:which + 1] = turned.astype(jnp.int32)
+            for first in range(0, sz.cells, LANES):
+                row = jnp.broadcast_to(turned[:, first:first + LANES], (LANES, LANES))
+                start = which * sz.cells + first
+                cols[layer][start:start + LANES] = jnp.transpose(row).astype(jnp.int32)
 
     barrier = pltpu.get_barrier_semaphore()
 
@@ -101,7 +128,8 @@
         )
         return carry
 
-    lax.fori_loop(1, peers, greet, 0)
+    lax.fori_loop(1, peers, greet, 0, unroll=8)
+    local_work(ENC)
     pl.semaphore_wait(barrier, peers - 1)
 
     def ask(step, carry):
@@ -113,7 +141,7 @@
         ).start()
         return carry
 
-    lax.fori_loop(1, peers, ask, 0)
+    lax.fori_loop(1, peers, ask, 0, unroll=8)
     asked[0] = ask_ref[me]
 
     def send(phase, start, stop):
@@ -125,7 +153,7 @@
             ).start()
             return carry
 
-        lax.fori_loop(max(start, 1), stop, one, 0)
+        lax.fori_loop(max(start, 1), stop, one, 0, unroll=8)
         if start == 0:
             landed[phase - 1, 0] = stage[phase - 1, 0]
 
@@ -135,20 +163,6 @@
 
     def wait_rows(phase):
         wait(recv_sem.at[phase], landed.at[phase - 1], peers - 1)
-
-    for layer in (ENC, DEC):
-        def cell_part(index, layer=layer):
-            span = rows_of(index, tile)
-            base[layer, span] = dot(grid_ref[span], w1_ref[layer, :256]) + bias_ref[layer:layer + 1]
-
-        loop(sz.cells // tile, cell_part)
-
-        def column(index, layer=layer):
-            row = pack_refs[layer][pl.ds(index, 1), :].astype(F32)
-            square = jnp.transpose(jnp.broadcast_to(row, (LANES, LANES)))
-            cols[layer][rows_of(index, LANES)] = square.astype(jnp.int32)
-
-        loop(sz.fanout[layer] * sz.cells // LANES, column)
 
     wait(recv_sem.at[0], asked, peers - 1)
     wide = asked[...].astype(F32)
@@ -193,7 +207,9 @@
         slot_sum[...] = jnp.zeros_like(slot_sum)
 
         def add(index):
-            row = jnp.broadcast_to(row_refs[layer][pl.ds(index, 1), :], (chunk, tile))
+            each = sz.cells // tile
+            span = pl.ds(pl.multiple_of(lax.rem(index, each) * tile, tile), tile)
+            row = jnp.broadcast_to(rows[layer][pl.ds(index // each, 1), span], (chunk, tile))
             sub = lax.broadcasted_iota(jnp.int32, (chunk, tile), 0) + start
             slot_sum[...] += dot(one_hot(row == sub), edge_low[rows_of(index, tile)])
 
@@ -202,7 +218,7 @@
     def cells_of(layer, index):
         return lax.rem(index, sz.cells // tile) * tile
 
-    fine = min(128, tile)
+    fine = min(1024, tile)
 
     def first_half(layer, index, hid_ref, hid_base):
         xm[...] = gather(layer, index).astype(BF16)
@@ -264,7 +280,8 @@
         low = (total - high.astype(F32)).astype(BF16)
         weight = w1_ref[layer, 256:]
         stage[phase - 1, start // 8:(start + chunk) // 8] = to_blocks(dot_nt(high, weight) + dot_nt(low, weight))
-        send(phase, start // 8, (start + chunk) // 8)
+        if layer == DEC:
+            send(phase, start // 8, (start + chunk) // 8)
         rows = table[start:start + chunk]
         parts[256:512] += dot_tn(rows, high) + dot_tn(rows, low)
 
@@ -280,9 +297,6 @@
 
         loop(sz.cells // tile, one)
 
-    def owner_of(layer, block):
-        return block if layer == ENC else peers - 1 - block
-
     def clear_parts():
         parts[...] = jnp.zeros_like(parts)
         part_vec[...] = jnp.zeros_like(part_vec)
@@ -295,65 +309,95 @@
                 for which in range(3) for side in range(2)
             ]
         ).astype(PART_WIRE[layer])
-        per = sz.per_owner
         pieces = [jnp.sum(part_vec[which], axis=0, keepdims=True) for which in range(3)]
         halves = [piece[:, LANES * side:LANES * side + LANES] for piece in pieces for side in range(2)]
         last = jnp.concatenate(halves + [jnp.zeros((10, LANES), F32)], axis=0).astype(PART_WIRE[layer])
-        for block in range(96):
-            rs_src[layer][block // per, (block % per) * 16:(block % per) * 16 + 16] = flat[block]
-        rs_src[layer][96 // per, (96 % per) * 16:(96 % per) * 16 + 16] = last
-        for block in range(97, sz.owners * per):
-            rs_src[layer][block // per, (block % per) * 16:(block % per) * 16 + 16] = jnp.zeros((16, LANES), PART_WIRE[layer])
-
-        def one(block):
-            target = owner_of(layer, block)
-
-            @pl.when(target != me)
+        own = sz.active * sz.piece
+        src = near_src[layer]
+        for first in range(0, 96, own):
+            stop = min(first + own, 96)
+            src[first // own, :stop - first] = flat[first:stop]
+        src[96 // own, 96 % own] = last
+        for block in range(97, sz.near * own):
+            src[block // own, block % own] = jnp.zeros((16, LANES), PART_WIRE[layer])
+        near_land[layer][member] = src[member]
+
+        def one(step, carry):
+            other = lax.rem(member + step, sz.near)
+            part_copy(layer, 0, src.at[other], near_land[layer].at[member], group * sz.near + other)
+            return carry
+
+        lax.fori_loop(1, sz.near, one, 0)
+
+    def part_copy(layer, stage_of, src, dst, target):
+        pltpu.make_async_remote_copy(
+            src_ref=src, dst_ref=dst,
+            send_sem=part_send.at[layer, stage_of], recv_sem=part_recv.at[layer, stage_of],
+            device_id=place(target), device_id_type=pl.DeviceIdType.MESH,
+        ).start()
+
+    def reduce_near(layer):
+        wait(part_recv.at[layer, 0], near_land[layer], sz.near - 1)
+        total = near_land[layer][0].astype(F32)
+        for index in range(1, sz.near):
+            total = total + near_land[layer][index].astype(F32)
+        far_src[layer][...] = total.reshape(sz.active, sz.piece, 16, LANES)
+
+        def one(index):
+            @pl.when(index != group)
             def _():
-                pltpu.make_async_remote_copy(
-                    src_ref=rs_src[layer].at[block], dst_ref=rs_land[layer].at[me],
-                    send_sem=rs_send.at[layer], recv_sem=rs_recv.at[layer],
-                    device_id=place(target), device_id_type=pl.DeviceIdType.MESH,
-                ).start()
-
-        loop(sz.owners, one)
-
-    def sum_parts(layer):
-        mine = owner_of(layer, me)
-
-        @pl.when(mine < sz.owners)
+                part_copy(layer, 1, far_src[layer].at[index], far_land[layer].at[group], index * sz.near + member)
+
+        loop(sz.active, one)
+
+    def reduce_far(layer):
+        @pl.when(group < sz.active)
         def _():
-            rs_land[layer][me] = rs_src[layer][mine]
-            wait(rs_recv.at[layer], rs_land[layer], peers - 1)
+            far_land[layer][group] = far_src[layer][group]
+            wait(part_recv.at[layer, 1], far_land[layer], sz.far - 1)
             scale = 1.0 / math.sqrt(sz.fanout[layer] * sz.cells * peers)
-            total = (jnp.sum(rs_land[layer][...].astype(F32), axis=0) * scale).astype(PART_WIRE[layer])
-            ag_src[layer][...] = total
-            ag_land[layer][mine] = total
+            far_sum[layer][group] = (jnp.sum(far_land[layer][...], axis=0) * scale).astype(PART_WIRE[layer])
 
             def one(step, carry):
-                pltpu.make_async_remote_copy(
-                    src_ref=ag_src[layer], dst_ref=ag_land[layer].at[mine],
-                    send_sem=ag_send.at[layer], recv_sem=ag_recv.at[layer],
-                    device_id=place(lax.rem(me + step, peers)), device_id_type=pl.DeviceIdType.MESH,
-                ).start()
+                other = lax.rem(group + step, sz.far)
+                part_copy(layer, 2, far_sum[layer].at[group], far_sum[layer].at[group], other * sz.near + member)
                 return carry
 
-            lax.fori_loop(1, peers, one, 0)
+            lax.fori_loop(1, sz.far, one, 0)
+
+    def spread_near(layer):
+        @pl.when(group < sz.active)
+        def _():
+            wait(part_recv.at[layer, 2], far_sum[layer], sz.active - 1)
+
+        @pl.when(group >= sz.active)
+        def _():
+            wait(part_recv.at[layer, 2], far_sum[layer], sz.active)
+
+        near_sum[layer][member] = far_sum[layer][...]
+
+        def one(step, carry):
+            other = lax.rem(member + step, sz.near)
+            part_copy(layer, 3, far_sum[layer], near_sum[layer].at[member], group * sz.near + other)
+            return carry
+
+        lax.fori_loop(1, sz.near, one, 0)
 
     def finish_parts(layer):
-        mine = owner_of(layer, me)
-        @pl.when(mine >= sz.owners)
+        wait(part_recv.at[layer, 3], near_sum[layer], sz.near - 1)
+        wait(part_send.at[layer, 0], near_land[layer], sz.near - 1)
+        wait(part_send.at[layer, 3], near_sum[layer], sz.near - 1)
+
+        @pl.when(group < sz.active)
         def _():
-            wait(ag_recv.at[layer], ag_land[layer], sz.owners)
-            wait(rs_send.at[layer], rs_src[layer], sz.owners)
-
-        @pl.when(mine < sz.owners)
+            wait(part_send.at[layer, 1], far_src[layer], sz.active - 1)
+            wait(part_send.at[layer, 2], far_wide[layer], sz.far - 1)
+
+        @pl.when(group >= sz.active)
         def _():
-            wait(ag_recv.at[layer], ag_land[layer], sz.owners - 1)
-            wait(rs_send.at[layer], rs_src[layer], sz.owners - 1)
-            wait(ag_send.at[layer], rs_land[layer], peers - 1)
-
-        flat = ag_land[layer][...].astype(F32).reshape(sz.owners * sz.per_owner, 16, LANES)
+            wait(part_send.at[layer, 1], far_src[layer], sz.active)
+
+        flat = near_sum[layer][...].astype(F32).reshape(sz.near * sz.active * sz.piece, 16, LANES)
         matrix = [
             jnp.concatenate(
                 [flat[32 * which + 16 * side:32 * which + 16 * side + 16].reshape(256, LANES) for side in range(2)],
@@ -369,10 +413,11 @@
             out[layer:layer + 1] = jnp.concatenate([last[2 * which:2 * which + 1], last[2 * which + 1:2 * which + 2]], axis=1)
 
     serve(1, lat_ref)
+    local_work(DEC)
     clear_parts()
     grid_out[...] = cot_ref[...].astype(F32)
     fetch(1)
-    broad = min(256, tile)
+    broad = min(1024, tile)
 
     def encode(index):
         first_half(ENC, index, hidden, index * tile)
@@ -434,8 +479,9 @@
     loop(sz.mesh_rows // sz.own_rows, make_mid_grad)
     serve(5, mid)
     clear_parts()
-    sum_parts(DEC)
+    reduce_near(DEC)
     fetch(5)
+    reduce_far(DEC)
 
     def encode_back(index):
         pre[...] = gather(ENC, index)
@@ -451,24 +497,43 @@
         second_back(ENC, index, hidden, index * tile)
 
     loop(sz.fanout[ENC] * sz.cells // tile, encode_back)
+    spread_near(DEC)
+    cell_back(ENC)
     table[...] = from_blocks(landed[0]).astype(BF16)
     send_slot_grads(ENC, 6)
-    cell_back(ENC)
     send_parts(ENC)
-
+    for start in range(0, slots, chunk):
+        send(6, start // 8, (start + chunk) // 8)
+    finish_parts(DEC)
+    reduce_near(ENC)
     fetch(6)
+    reduce_far(ENC)
 
     def make_mesh_out(index):
         span = rows_of(index, sz.own_rows)
         mesh_out[span] = mid_grad[span] + returned(6, index * sz.own_rows, span)
 
-    loop(sz.mesh_rows // sz.own_rows, make_mesh_out)
-    sum_parts(ENC)
-    finish_parts(DEC)
+    loop(sz.mesh_rows // sz.own_rows - 1, make_mesh_out)
+    spread_near(ENC)
+    make_mesh_out(sz.mesh_rows // sz.own_rows - 1)
     finish_parts(ENC)
     wait(send_sem.at[0], asked, peers - 1)
     for phase in range(1, 7):
         wait(send_sem.at[phase], landed.at[phase - 1], peers - 1)
+
+
+def hand_over(count, *refs):
+    given, taken, held = refs[:count], refs[count:2 * count], refs[2 * count:3 * count]
+    sems = refs[-1]
+    reads = [pltpu.make_async_copy(given[index], held[index], sems.at[0, index]) for index in range(count)]
+    writes = [pltpu.make_async_copy(held[index], taken[index], sems.at[1, index]) for index in range(count)]
+    for copy in reads:
+        copy.start()
+    for read, write in zip(reads, writes):
+        read.wait()
+        write.start()
+    for copy in writes:
+        copy.wait()
 
 
 def per_device(
@@ -480,12 +545,9 @@
     mesh_rows = mesh_node_latents.shape[0]
     sz = Sizes(slabs, bricks, cells, mesh_rows, enc_slots.shape[0], dec_slots.shape[0])
     peers, slots, tile = sz.peers, sz.slots, sz.tile
-    me = lax.axis_index("slab") * bricks + lax.axis_index("brick")
     positions = lax.broadcasted_iota(jnp.int32, (peers, 8), 1)
     asking = jnp.where(positions < counts.reshape(peers, 1), requests, -1)
     asking = jnp.pad(asking, ((0, 0), (0, LANES - 8))).reshape(peers, 1, LANES)
-    enc_turned = lax.rem(enc_slots - 8 * me + slots, slots)
-    dec_turned = lax.rem(dec_slots - 8 * me + slots, slots)
     enc_edges, dec_edges = sz.fanout[ENC] * cells, sz.fanout[DEC] * cells
     vmem = pl.BlockSpec(memory_space=pltpu.VMEM)
     outs = [
@@ -496,11 +558,13 @@
         )
     ]
     dma = pltpu.SemaphoreType.DMA
-    per = sz.per_owner
+    own = sz.active * sz.piece
     scratch = [
         pltpu.VMEM((peers, 1, LANES), jnp.int32),
         pltpu.VMEM((slots, LANES), jnp.int32),
         pltpu.VMEM((8, slots), jnp.int32),
+        pltpu.VMEM((sz.fanout[ENC], cells), jnp.int32),
+        pltpu.VMEM((sz.fanout[DEC], cells), jnp.int32),
         pltpu.VMEM((enc_edges, LANES), jnp.int32),
         pltpu.VMEM((dec_edges, LANES), jnp.int32),
         pltpu.VMEM((2, cells, features), F32),
@@ -521,17 +585,20 @@
         pltpu.VMEM((sz.chunk, features), F32),
         pltpu.VMEM((3 * features, features), F32),
         pltpu.VMEM((3, 8, features), F32),
-        *[pltpu.VMEM((sz.owners, per * 16, LANES), kind) for kind in PART_WIRE],
-        *[pltpu.VMEM((peers, per * 16, LANES), kind) for kind in PART_WIRE],
-        *[pltpu.VMEM((per * 16, LANES), kind) for kind in PART_WIRE],
-        *[pltpu.VMEM((sz.owners, per * 16, LANES), kind) for kind in PART_WIRE],
-        dma((7,)), dma((7,)), dma((2,)), dma((2,)), dma((2,)), dma((2,)),
+        *[pltpu.VMEM((sz.near, own, 16, LANES), kind) for kind in PART_WIRE],
+        *[pltpu.VMEM((sz.near, own, 16, LANES), kind) for kind in PART_WIRE],
+        *[pltpu.VMEM((sz.active, sz.piece, 16, LANES), F32) for kind in PART_WIRE],
+        *[pltpu.VMEM((sz.far, sz.piece, 16, LANES), F32) for kind in PART_WIRE],
+        *[pltpu.VMEM((sz.active, sz.piece, 16, LANES), kind) for kind in PART_WIRE],
+        *[pltpu.VMEM((sz.near, sz.active, sz.piece, 16, LANES), kind) for kind in PART_WIRE],
+        *[pltpu.VMEM((sz.far, sz.piece, 16, LANES), kind) for kind in PART_WIRE],
+        dma((7,)), dma((7,)), dma((2, 4)), dma((2, 4)),
     ]
-    return tuple(
+    made = tuple(
         pl.pallas_call(
             functools.partial(kernel, sz),
             out_shape=outs,
-            in_specs=[vmem] * 14,
+            in_specs=[vmem] * 12,
             out_specs=[vmem] * 7,
             scratch_shapes=scratch,
             compiler_params=pltpu.CompilerParams(
@@ -540,9 +607,18 @@
         )(
             grid_latent, mesh_node_latents, grid_cot, mesh_cotangent, w_first, w_second,
             biases, ln_gain, ln_shift, asking,
-            enc_turned.reshape(enc_edges // tile, tile), dec_turned.reshape(dec_edges // tile, tile),
-            enc_turned.reshape(enc_edges // LANES, LANES), dec_turned.reshape(dec_edges // LANES, LANES),
+            enc_slots, dec_slots,
         )
+    )
+    anywhere = pl.BlockSpec(memory_space=pl.ANY)
+    return tuple(
+        pl.pallas_call(
+            functools.partial(hand_over, len(made)),
+            out_shape=outs,
+            in_specs=[anywhere] * len(made),
+            out_specs=[anywhere] * len(made),
+            scratch_shapes=[pltpu.VMEM(out.shape, F32) for out in outs] + [dma((2, len(made)))],
+        )(*made)
     )
 
 

time: 203 us -> 163 us (0.80)
  Pallas kernels: 187 us -> 160 us
  local copies, waits for them, and re-layouts: 12.4 us -> 1.43 us
    pallas_call x1, Pallas kernels: 187 us -> 156 us  [per_device(): pl.pallas_call(functools.partial(kernel, sz), out_shape=outs, in_specs=[v...]
    unnamed x20 -> x1, local copies, waits for them, and re-layouts: 9.25 us -> 0.79 us
    pallas_call x0 -> x1, Pallas kernels: none -> 4.07 us  [per_device(): pl.pallas_call(functools.partial(hand_over, len(made)), out_shape=outs, i...]
    reshape x4 -> x0, local copies, waits for them, and re-layouts: 2.5 us -> none  [the longest x1 0.63 us: per_device(): dec_turned.reshape(dec_edges // tile, tile)]
where the time goes in v3:
time: 163 us
  Pallas kernels  160 us (98%)
    pallas_call x1, Pallas kernels, per_device(): pl.pallas_call(functools.partial(kernel, sz), out_shape=outs, in_specs=[v...  156 us
    pallas_call x1, Pallas kernels, per_device(): pl.pallas_call(functools.partial(hand_over, len(made)), out_shape=outs, i...  4.07 us

profile of v3, /device:TPU:1, one launch (start us, length us, event | category | flops | bytes accessed | tf_op | source)
XLA Modules:
  0.0 163.3 jit_solution(13678399375882585646)
XLA Ops:
  0.6 0.8 copy.20
  1.4 0.7 fusion
  2.2 0.6 pad.4
  2.8 156.3 %shard_map.180 = (f32[2048,256]{1,0:T(8,128)}, f32[1536,256]{1,0:T(8,128)}, f32[2,512,256]{2,1,0:T(8,128)}, f32[2,256,256]{2,1,0:T(8,128)}, f32[2,256]{1,0:T(2,1...) custom-call(bf16[2048,256]{1,0:T(8,128)(2,1)} %grid_ref.1, bf16[1536,256]{1,0:T(8,128)(2,1)} %lat_ref.1, ...), custom_call_target="tpu_custom_call" | custom-call | tf_op jit(solution)/shard_map/pallas_call | solution.py:598
  159.1 4.1 %shard_map.181 = (f32[2048,256]{1,0:T(8,128)}, f32[1536,256]{1,0:T(8,128)}, f32[2,512,256]{2,1,0:T(8,128)}, f32[2,256,256]{2,1,0:T(8,128)}, f32[2,256]{1,0:T(2,1...) custom-call(f32[2048,256]{1,0:T(8,128)} %get-tuple-element.14.refs_0_, f32[1536,256]{1,0:T(8,128)} %get-tuple-element.15.refs_1_, ...), custom_call_target="tpu_custom_call" | custom-call | tf_op jit(solution)/shard_map/pallas_call | solution.py:615

commit v4 on v3

--- a/solution.py
+++ b/solution.py
@@ -13,6 +13,8 @@
 BF16 = jnp.bfloat16
 F32 = jnp.float32
 ENC, DEC = 0, 1
+NEAR = (1, 8)
+PART_SUM_WIRE = (BF16, BF16)
 PART_WIRE = (BF16, F32)
 
 
@@ -57,11 +59,12 @@
         self.tile = min(1024, cells)
         self.chunk = min(512, self.slots)
         self.own_rows = math.gcd(512, mesh_rows)
-        self.near = bricks // 4 if bricks >= 16 else 4
-        self.far = self.peers // self.near
-        share = -(-97 // self.near)
-        self.piece = -(-share // self.far)
-        self.active = -(-share // self.piece)
+        self.half = 49
+        self.near = NEAR if self.peers >= 128 else (2, 4)
+        self.far = tuple(self.peers // 2 // near for near in self.near)
+        share = tuple(-(-self.half // near) for near in self.near)
+        self.piece = tuple(-(-each // far) for each, far in zip(share, self.far))
+        self.active = tuple(-(-each // piece) for each, piece in zip(share, self.piece))
 
 
 def kernel(
@@ -71,20 +74,23 @@
     grid_out, mesh_out, w1_out, w2_out, bias_out, gain_out, shift_out,
     asked, ask_col, ask_row, enc_row, dec_row, enc_col, dec_col, base, table, stage, landed,
     pre, xm, outer_low, hidden, deriv, normed, invstd, edge_low,
-    cell_sum, mid, mid_grad, slot_sum, parts, part_vec,
-    near_src_enc, near_src_dec, near_land_enc, near_land_dec, far_src_enc, far_src_dec, far_land_enc, far_land_dec,
-    far_sum_enc, far_sum_dec, near_sum_enc, near_sum_dec, far_wide_enc, far_wide_dec,
+    cell_sum, mid, slot_sum, parts, part_vec,
+    pair_src_enc, pair_src_dec, pair_land_enc, pair_land_dec, near_src_enc, near_src_dec,
+    near_land_enc, near_land_dec, far_src_enc, far_src_dec, far_land_enc, far_land_dec,
+    far_sum_enc, far_sum_dec, near_sum_enc, near_sum_dec, pair_sum_enc, pair_sum_dec, far_wide_enc, far_wide_dec,
     send_sem, recv_sem, part_send, part_recv,
 ):
     peers, slots, tile, chunk = sz.peers, sz.slots, sz.tile, sz.chunk
     me = lax.axis_index("slab") * sz.bricks + lax.axis_index("brick")
     row_refs, rows, cols = (enc_row_ref, dec_row_ref), (enc_row, dec_row), (enc_col, dec_col)
 
+    pair_src, pair_land = (pair_src_enc, pair_src_dec), (pair_land_enc, pair_land_dec)
     near_src, near_land = (near_src_enc, near_src_dec), (near_land_enc, near_land_dec)
     far_src, far_land = (far_src_enc, far_src_dec), (far_land_enc, far_land_dec)
-    far_sum, near_sum = (far_sum_enc, far_sum_dec), (near_sum_enc, near_sum_dec)
+    far_sum, near_sum, pair_sum = (far_sum_enc, far_sum_dec), (near_sum_enc, near_sum_dec), (pair_sum_enc, pair_sum_dec)
     far_wide = (far_wide_enc, far_wide_dec)
-    group, member = me // sz.near, lax.rem(me, sz.near)
+    chip, core = me // 2, lax.rem(me, 2)
+    bases = (base, grid_out)
 
     def place(peer):
         return (peer // sz.bricks, lax.rem(peer, sz.bricks))
@@ -98,6 +104,19 @@
             return carry
 
         lax.fori_loop(0, count, step, 0)
+
+    def in_pairs(count, body):
+        def both(index):
+            running = [body(2 * index + side, side) for side in range(2)]
+            for _ in zip(*running):
+                pass
+
+        if count % 2:
+            for index in range(count):
+                for _ in body(index, 0):
+                    pass
+        else:
+            loop(count // 2, both)
 
     def rows_of(index, size):
         if isinstance(index, int):
@@ -107,7 +126,7 @@
     def local_work(layer):
         def cell_part(index):
             span = rows_of(index, tile)
-            base[layer, span] = dot(grid_ref[span], w1_ref[layer, :256]) + bias_ref[layer:layer + 1]
+            bases[layer][span] = dot(grid_ref[span], w1_ref[layer, :256]) + bias_ref[layer:layer + 1]
 
         loop(sz.cells // tile, cell_part)
         for which in range(sz.fanout[layer]):
@@ -117,7 +136,7 @@
             for first in range(0, sz.cells, LANES):
                 row = jnp.broadcast_to(turned[:, first:first + LANES], (LANES, LANES))
                 start = which * sz.cells + first
-                cols[layer][start:start + LANES] = jnp.transpose(row).astype(jnp.int32)
+                cols[layer][start:start + LANES] = jnp.transpose(row).astype(jnp.int16)
 
     barrier = pltpu.get_barrier_semaphore()
 
@@ -147,7 +166,7 @@
     def send(phase, start, stop):
         def one(step, carry):
             pltpu.make_async_remote_copy(
-                src_ref=stage.at[phase - 1, step], dst_ref=landed.at[phase - 1, peers - step],
+                src_ref=stage.at[(phase - 1) % 3, step], dst_ref=landed.at[phase - 1, peers - step],
                 send_sem=send_sem.at[phase], recv_sem=recv_sem.at[phase],
                 device_id=place(lax.rem(me + step, peers)), device_id_type=pl.DeviceIdType.MESH,
             ).start()
@@ -155,7 +174,7 @@
 
         lax.fori_loop(max(start, 1), stop, one, 0, unroll=8)
         if start == 0:
-            landed[phase - 1, 0] = stage[phase - 1, 0]
+            landed[phase - 1, 0] = stage[(phase - 1) % 3, 0]
 
     def wait(sem, ref, count):
         span = ref.at[pl.ds(0, count)]
@@ -163,6 +182,7 @@
 
     def wait_rows(phase):
         wait(recv_sem.at[phase], landed.at[phase - 1], peers - 1)
+        wait(send_sem.at[phase], landed.at[phase - 1], peers - 1)
 
     wait(recv_sem.at[0], asked, peers - 1)
     wide = asked[...].astype(F32)
@@ -183,7 +203,7 @@
             chosen = jnp.concatenate(
                 [one_hot(column == lanes + first) for first in range(0, sz.mesh_rows, LANES)], axis=1
             )[:, :sz.mesh_rows]
-            stage[phase - 1, start // 8:(start + chunk) // 8] = to_blocks(dot(chosen, source[...]))
+            stage[(phase - 1) % 3, start // 8:(start + chunk) // 8] = to_blocks(dot(chosen, source[...]))
             send(phase, start // 8, (start + chunk) // 8)
 
     def fetch(phase):
@@ -199,7 +219,7 @@
         column = cols[layer][rows_of(index, tile)]
         lanes = lax.broadcasted_iota(jnp.int32, (tile, LANES), 1)
         chosen = jnp.concatenate(
-            [one_hot(column == lanes + first) for first in range(0, slots, LANES)], axis=1
+            [one_hot(column == (lanes + first).astype(jnp.int16)) for first in range(0, slots, LANES)], axis=1
         )
         return dot(chosen, table[...])
 
@@ -220,21 +240,25 @@
 
     fine = min(1024, tile)
 
-    def first_half(layer, index, hid_ref, hid_base):
-        xm[...] = gather(layer, index).astype(BF16)
-        pre[...] = dot(xm[...], w1_ref[layer, 256:])
+    def first_half(layer, index, hid_ref, hid_base, side):
+        xm[side] = gather(layer, index).astype(BF16)
+        yield
+        pre[side] = dot(xm[side], w1_ref[layer, 256:])
+        yield
         cell = cells_of(layer, index)
 
         def act(part):
             span = rows_of(part, fine)
-            x = pre[span] + base[layer, pl.ds(pl.multiple_of(cell + part * fine, fine), fine)]
+            x = pre[side, span] + bases[layer][pl.ds(pl.multiple_of(cell + part * fine, fine), fine)]
             gate = 0.5 * jnp.tanh(0.5 * x) + 0.5
             value = x * gate
             hid_ref[pl.ds(pl.multiple_of(hid_base + part * fine, fine), fine)] = value.astype(BF16)
             deriv[pl.ds(pl.multiple_of(hid_base + part * fine, fine), fine)] = gate + value * (1.0 - gate)
 
         loop(tile // fine, act)
-        pre[...] = dot(hid_ref[pl.ds(pl.multiple_of(hid_base, tile), tile)], w2_ref[layer])
+        yield
+        pre[side] = dot(hid_ref[pl.ds(pl.multiple_of(hid_base, tile), tile)], w2_ref[layer])
+        yield
 
     def normalise(x):
         center = x - jnp.mean(x, axis=-1, keepdims=True)
@@ -251,23 +275,25 @@
         )
         return out, fold(weighed), fold(cot)
 
-    def accumulate(slot, value):
-        part_vec[slot] += value
-
-    def second_back(layer, index, hid_ref, hid_base):
-        parts[512:768] += dot_tn(hid_ref[pl.ds(pl.multiple_of(hid_base, tile), tile)], outer_low[...])
-        pre[...] = dot_nt(outer_low[...], w2_ref[layer])
+    def accumulate(side, slot, value):
+        part_vec[side, slot] += value
+
+    def second_back(layer, index, hid_ref, hid_base, side):
+        parts[512:768] += dot_tn(hid_ref[pl.ds(pl.multiple_of(hid_base, tile), tile)], outer_low[side])
+        pre[side] = dot_nt(outer_low[side], w2_ref[layer])
+        yield
         cell = cells_of(layer, index)
 
         def act(part):
-            grad = pre[rows_of(part, fine)] * deriv[pl.ds(pl.multiple_of(hid_base + part * fine, fine), fine)]
-            accumulate(0, fold(grad))
+            grad = pre[side, rows_of(part, fine)] * deriv[pl.ds(pl.multiple_of(hid_base + part * fine, fine), fine)]
+            accumulate(side, 0, fold(grad))
             low = grad.astype(BF16)
             edge_low[pl.ds(pl.multiple_of(index * tile + part * fine, fine), fine)] = low
             span = pl.ds(pl.multiple_of(cell + part * fine, fine), fine)
             cell_sum[span] += low.astype(F32)
 
         loop(tile // fine, act)
+        yield
 
     def send_slot_grads(layer, phase):
         for start in range(0, slots, chunk):
@@ -279,7 +305,7 @@
         high = total.astype(BF16)
         low = (total - high.astype(F32)).astype(BF16)
         weight = w1_ref[layer, 256:]
-        stage[phase - 1, start // 8:(start + chunk) // 8] = to_blocks(dot_nt(high, weight) + dot_nt(low, weight))
+        stage[(phase - 1) % 3, start // 8:(start + chunk) // 8] = to_blocks(dot_nt(high, weight) + dot_nt(low, weight))
         if layer == DEC:
             send(phase, start // 8, (start + chunk) // 8)
         rows = table[start:start + chunk]
@@ -292,7 +318,8 @@
             high = total.astype(BF16)
             low = (total - high.astype(F32)).astype(BF16)
             weight, rows = w1_ref[layer, :256], grid_ref[span]
-            grid_out[span] += dot_nt(high, weight) + dot_nt(low, weight)
+            before = cot_ref[span].astype(F32) if layer == DEC else grid_out[span]
+            grid_out[span] = before + dot_nt(high, weight) + dot_nt(low, weight)
             parts[0:256] += dot_tn(rows, high) + dot_tn(rows, low)
 
         loop(sz.cells // tile, one)
@@ -308,96 +335,156 @@
                 parts[256 * which:256 * which + 256, LANES * side:LANES * side + LANES].reshape(16, 16, LANES)
                 for which in range(3) for side in range(2)
             ]
-        ).astype(PART_WIRE[layer])
-        pieces = [jnp.sum(part_vec[which], axis=0, keepdims=True) for which in range(3)]
+        )
+        pieces = [jnp.sum(part_vec[0, which] + part_vec[1, which], axis=0, keepdims=True) for which in range(3)]
         halves = [piece[:, LANES * side:LANES * side + LANES] for piece in pieces for side in range(2)]
-        last = jnp.concatenate(halves + [jnp.zeros((10, LANES), F32)], axis=0).astype(PART_WIRE[layer])
-        own = sz.active * sz.piece
-        src = near_src[layer]
-        for first in range(0, 96, own):
-            stop = min(first + own, 96)
-            src[first // own, :stop - first] = flat[first:stop]
-        src[96 // own, 96 % own] = last
-        for block in range(97, sz.near * own):
-            src[block // own, block % own] = jnp.zeros((16, LANES), PART_WIRE[layer])
-        near_land[layer][member] = src[member]
-
-        def one(step, carry):
-            other = lax.rem(member + step, sz.near)
-            part_copy(layer, 0, src.at[other], near_land[layer].at[member], group * sz.near + other)
-            return carry
-
-        lax.fori_loop(1, sz.near, one, 0)
-
-    def part_copy(layer, stage_of, src, dst, target):
+        last = jnp.concatenate(halves + [jnp.zeros((10, LANES), F32)], axis=0)
+        pair_src[layer][0] = flat[:sz.half]
+        pair_src[layer][1, :96 - sz.half] = flat[sz.half:]
+        pair_src[layer][1, 96 - sz.half] = last
+        pair_src[layer][1, 97 - sz.half] = jnp.zeros((16, LANES), F32)
+        part_copy(layer, 0, pair_src[layer].at[1 - core], pair_land[layer], chip, 1 - core)
+
+    def part_copy(layer, stage_of, src, dst, to_chip, to_core):
         pltpu.make_async_remote_copy(
             src_ref=src, dst_ref=dst,
             send_sem=part_send.at[layer, stage_of], recv_sem=part_recv.at[layer, stage_of],
-            device_id=place(target), device_id_type=pl.DeviceIdType.MESH,
+            device_id=place(to_chip * 2 + to_core), device_id_type=pl.DeviceIdType.MESH,
         ).start()
 
+    def whole(sem, ref):
+        pltpu.make_async_copy(ref, ref, sem).wait()
+
+    def split(layer):
+        return chip // sz.near[layer], lax.rem(chip, sz.near[layer])
+
+    def to_far(layer, total):
+        far_src[layer][...] = total.reshape(far_src[layer].shape).astype(far_src[layer].dtype)
+        group, member = split(layer)
+
+        def one(step, carry):
+            other = lax.rem(group + step, sz.far[layer])
+
+            @pl.when(other < sz.active[layer])
+            def _():
+                part_copy(
+                    layer, 2, far_src[layer].at[other], far_land[layer].at[group],
+                    other * sz.near[layer] + member, core,
+                )
+
+            return carry
+
+        lax.fori_loop(1, sz.far[layer], one, 0)
+
+    def reduce_pair(layer):
+        whole(part_recv.at[layer, 0], pair_land[layer])
+        total = pair_src[layer][core] + pair_land[layer][...]
+        near = sz.near[layer]
+        if near == 1:
+            to_far(layer, total)
+            return
+        group, member = split(layer)
+        own = sz.active[layer] * sz.piece[layer]
+        for index in range(near):
+            count = max(0, min(own, sz.half - index * own))
+            if count:
+                near_src[layer][index, :count] = total[index * own:index * own + count].astype(near_src[layer].dtype)
+            if count < own:
+                near_src[layer][index, count:] = jnp.zeros((own - count, 16, LANES), near_src[layer].dtype)
+        near_land[layer][member] = near_src[layer][member]
+
+        def one(step, carry):
+            other = lax.rem(member + step, near)
+            part_copy(layer, 1, near_src[layer].at[other], near_land[layer].at[member], group * near + other, core)
+            return carry
+
+        lax.fori_loop(1, near, one, 0)
+
     def reduce_near(layer):
-        wait(part_recv.at[layer, 0], near_land[layer], sz.near - 1)
+        if sz.near[layer] == 1:
+            return
+        wait(part_recv.at[layer, 1], near_land[layer], sz.near[layer] - 1)
         total = near_land[layer][0].astype(F32)
-        for index in range(1, sz.near):
+        for index in range(1, sz.near[layer]):
             total = total + near_land[layer][index].astype(F32)
-        far_src[layer][...] = total.reshape(sz.active, sz.piece, 16, LANES)
-
-        def one(index):
-            @pl.when(index != group)
-            def _():
-                part_copy(layer, 1, far_src[layer].at[index], far_land[layer].at[group], index * sz.near + member)
-
-        loop(sz.active, one)
+        to_far(layer, total)
 
     def reduce_far(layer):
-        @pl.when(group < sz.active)
+        group, member = split(layer)
+
+        @pl.when(group < sz.active[layer])
         def _():
             far_land[layer][group] = far_src[layer][group]
-            wait(part_recv.at[layer, 1], far_land[layer], sz.far - 1)
+            wait(part_recv.at[layer, 2], far_land[layer], sz.far[layer] - 1)
             scale = 1.0 / math.sqrt(sz.fanout[layer] * sz.cells * peers)
-            far_sum[layer][group] = (jnp.sum(far_land[layer][...], axis=0) * scale).astype(PART_WIRE[layer])
+            total = jnp.sum(far_land[layer][...].astype(F32), axis=0) * scale
+            far_sum[layer][group] = total.astype(PART_WIRE[layer])
 
             def one(step, carry):
-                other = lax.rem(group + step, sz.far)
-                part_copy(layer, 2, far_sum[layer].at[group], far_sum[layer].at[group], other * sz.near + member)
+                other = lax.rem(group + step, sz.far[layer])
+                part_copy(
+                    layer, 3, far_sum[layer].at[group], far_sum[layer].at[group],
+                    other * sz.near[layer] + member, core,
+                )
                 return carry
 
-            lax.fori_loop(1, sz.far, one, 0)
+            lax.fori_loop(1, sz.far[layer], one, 0)
+
+    def to_pair(layer):
+        pair_sum[layer][core] = near_sum[layer][...]
+        part_copy(layer, 5, near_sum[layer], pair_sum[layer].at[core], chip, 1 - core)
 
     def spread_near(layer):
-        @pl.when(group < sz.active)
+        group, member = split(layer)
+        active, near = sz.active[layer], sz.near[layer]
+
+        @pl.when(group < active)
         def _():
-            wait(part_recv.at[layer, 2], far_sum[layer], sz.active - 1)
-
-        @pl.when(group >= sz.active)
+            wait(part_recv.at[layer, 3], far_sum[layer], active - 1)
+
+        @pl.when(group >= active)
         def _():
-            wait(part_recv.at[layer, 2], far_sum[layer], sz.active)
+            wait(part_recv.at[layer, 3], far_sum[layer], active)
 
         near_sum[layer][member] = far_sum[layer][...]
+        if near == 1:
+            to_pair(layer)
+            return
 
         def one(step, carry):
-            other = lax.rem(member + step, sz.near)
-            part_copy(layer, 3, far_sum[layer], near_sum[layer].at[member], group * sz.near + other)
+            other = lax.rem(member + step, near)
+            part_copy(layer, 4, far_sum[layer], near_sum[layer].at[member], group * near + other, core)
             return carry
 
-        lax.fori_loop(1, sz.near, one, 0)
+        lax.fori_loop(1, near, one, 0)
+
+    def spread_pair(layer):
+        if sz.near[layer] > 1:
+            wait(part_recv.at[layer, 4], near_sum[layer], sz.near[layer] - 1)
+            to_pair(layer)
 
     def finish_parts(layer):
-        wait(part_recv.at[layer, 3], near_sum[layer], sz.near - 1)
-        wait(part_send.at[layer, 0], near_land[layer], sz.near - 1)
-        wait(part_send.at[layer, 3], near_sum[layer], sz.near - 1)
-
-        @pl.when(group < sz.active)
+        group, member = split(layer)
+        active, near = sz.active[layer], sz.near[layer]
+        whole(part_recv.at[layer, 5], near_sum[layer])
+        whole(part_send.at[layer, 5], near_sum[layer])
+        whole(part_send.at[layer, 0], pair_land[layer])
+        if near > 1:
+            wait(part_send.at[layer, 1], near_land[layer], near - 1)
+            wait(part_send.at[layer, 4], near_sum[layer], near - 1)
+
+        @pl.when(group < active)
         def _():
-            wait(part_send.at[layer, 1], far_src[layer], sz.active - 1)
-            wait(part_send.at[layer, 2], far_wide[layer], sz.far - 1)
-
-        @pl.when(group >= sz.active)
+            wait(part_send.at[layer, 2], far_src[layer], active - 1)
+            wait(part_send.at[layer, 3], far_wide[layer], sz.far[layer] - 1)
+
+        @pl.when(group >= active)
         def _():
-            wait(part_send.at[layer, 1], far_src[layer], sz.active)
-
-        flat = near_sum[layer][...].astype(F32).reshape(sz.near * sz.active * sz.piece, 16, LANES)
+            wait(part_send.at[layer, 2], far_src[layer], active)
+
+        sums = pair_sum[layer][...].astype(F32)
+        blocks = near * active * sz.piece[layer]
+        flat = jnp.concatenate([sums[side].reshape(blocks, 16, LANES)[:sz.half] for side in range(2)])
         matrix = [
             jnp.concatenate(
                 [flat[32 * which + 16 * side:32 * which + 16 * side + 16].reshape(256, LANES) for side in range(2)],
@@ -415,23 +502,23 @@
     serve(1, lat_ref)
     local_work(DEC)
     clear_parts()
-    grid_out[...] = cot_ref[...].astype(F32)
     fetch(1)
     broad = min(1024, tile)
 
-    def encode(index):
-        first_half(ENC, index, hidden, index * tile)
+    def encode(index, side):
+        yield from first_half(ENC, index, hidden, index * tile, side)
 
         def act(part):
             span = pl.ds(pl.multiple_of(index * tile + part * broad, broad), broad)
-            unit, inv = normalise(pre[rows_of(part, broad)])
+            unit, inv = normalise(pre[side, rows_of(part, broad)])
             normed[span] = unit
             invstd[span] = inv
             edge_low[span] = (unit * gain_ref[ENC:ENC + 1] + shift_ref[ENC:ENC + 1]).astype(BF16)
 
         loop(tile // broad, act)
-
-    loop(sz.fanout[ENC] * sz.cells // tile, encode)
+        yield
+
+    in_pairs(sz.fanout[ENC] * sz.cells // tile, encode)
     for start in range(0, slots, chunk):
         slot_sums(ENC, start)
         stage[1, start // 8:(start + chunk) // 8] = to_blocks(slot_sum[...])
@@ -447,23 +534,24 @@
     serve(3, mid)
     fetch(3)
 
-    def decode(index):
-        behind = sz.fanout[ENC] * sz.cells
-        first_half(DEC, index, hidden, behind)
+    def decode(index, side):
+        behind = sz.fanout[ENC] * sz.cells + side * tile
+        yield from first_half(DEC, index, hidden, behind, side)
         cell = cells_of(DEC, index)
 
         def act(part):
-            unit, inv = normalise(pre[rows_of(part, broad)])
+            unit, inv = normalise(pre[side, rows_of(part, broad)])
             cot = cot_ref[pl.ds(pl.multiple_of(cell + part * broad, broad), broad)].astype(F32)
             out, gain, shift = outer_back(DEC, unit, inv, cot)
-            accumulate(1, gain)
-            accumulate(2, shift)
-            outer_low[rows_of(part, broad)] = out.astype(BF16)
+            accumulate(side, 1, gain)
+            accumulate(side, 2, shift)
+            outer_low[side, rows_of(part, broad)] = out.astype(BF16)
 
         loop(tile // broad, act)
-        second_back(DEC, index, hidden, behind)
-
-    loop(sz.fanout[DEC] * sz.cells // tile, decode)
+        yield
+        yield from second_back(DEC, index, hidden, behind, side)
+
+    in_pairs(sz.fanout[DEC] * sz.cells // tile, decode)
     send_slot_grads(DEC, 4)
     cell_back(DEC)
     send_parts(DEC)
@@ -473,53 +561,60 @@
     def make_mid_grad(index):
         span = rows_of(index, sz.own_rows)
         total = mesh_cot_ref[span].astype(F32) + returned(4, index * sz.own_rows, span)
-        mid_grad[span] = total
+        mesh_out[span] = total
         mid[span] = total.astype(BF16)
 
     loop(sz.mesh_rows // sz.own_rows, make_mid_grad)
     serve(5, mid)
     clear_parts()
+    reduce_pair(DEC)
+    fetch(5)
     reduce_near(DEC)
-    fetch(5)
-    reduce_far(DEC)
-
-    def encode_back(index):
-        pre[...] = gather(ENC, index)
+
+    def encode_back(index, side):
+        pre[side] = gather(ENC, index)
+        yield
 
         def act(part):
             span = pl.ds(pl.multiple_of(index * tile + part * broad, broad), broad)
-            out, gain, shift = outer_back(ENC, normed[span], invstd[span], pre[rows_of(part, broad)])
-            accumulate(1, gain)
-            accumulate(2, shift)
-            outer_low[rows_of(part, broad)] = out.astype(BF16)
+            out, gain, shift = outer_back(ENC, normed[span], invstd[span], pre[side, rows_of(part, broad)])
+            accumulate(side, 1, gain)
+            accumulate(side, 2, shift)
+            outer_low[side, rows_of(part, broad)] = out.astype(BF16)
 
         loop(tile // broad, act)
-        second_back(ENC, index, hidden, index * tile)
-
-    loop(sz.fanout[ENC] * sz.cells // tile, encode_back)
+        yield
+        yield from second_back(ENC, index, hidden, index * tile, side)
+
+    tiles = sz.fanout[ENC] * sz.cells // tile
+    in_pairs(tiles // 2, encode_back)
+    reduce_far(DEC)
+    in_pairs(tiles - tiles // 2, lambda index, side: encode_back(index + tiles // 2, side))
     spread_near(DEC)
     cell_back(ENC)
     table[...] = from_blocks(landed[0]).astype(BF16)
     send_slot_grads(ENC, 6)
     send_parts(ENC)
+    spread_pair(DEC)
     for start in range(0, slots, chunk):
         send(6, start // 8, (start + chunk) // 8)
+        if start == 0:
+            reduce_pair(ENC)
     finish_parts(DEC)
+    fetch(6)
     reduce_near(ENC)
-    fetch(6)
     reduce_far(ENC)
 
     def make_mesh_out(index):
         span = rows_of(index, sz.own_rows)
-        mesh_out[span] = mid_grad[span] + returned(6, index * sz.own_rows, span)
+        mesh_out[span] += returned(6, index * sz.own_rows, span)
 
     loop(sz.mesh_rows // sz.own_rows - 1, make_mesh_out)
     spread_near(ENC)
     make_mesh_out(sz.mesh_rows // sz.own_rows - 1)
+    spread_pair(ENC)
     finish_parts(ENC)
     wait(send_sem.at[0], asked, peers - 1)
-    for phase in range(1, 7):
-        wait(send_sem.at[phase], landed.at[phase - 1], peers - 1)
 
 
 def hand_over(count, *refs):
@@ -558,41 +653,43 @@
         )
     ]
     dma = pltpu.SemaphoreType.DMA
-    own = sz.active * sz.piece
+    own = [sz.active[l] * sz.piece[l] for l in range(2)]
+    far_wire = [F32 if sz.near[l] > 1 else PART_SUM_WIRE[l] for l in range(2)]
     scratch = [
         pltpu.VMEM((peers, 1, LANES), jnp.int32),
         pltpu.VMEM((slots, LANES), jnp.int32),
         pltpu.VMEM((8, slots), jnp.int32),
         pltpu.VMEM((sz.fanout[ENC], cells), jnp.int32),
         pltpu.VMEM((sz.fanout[DEC], cells), jnp.int32),
-        pltpu.VMEM((enc_edges, LANES), jnp.int32),
-        pltpu.VMEM((dec_edges, LANES), jnp.int32),
-        pltpu.VMEM((2, cells, features), F32),
+        pltpu.VMEM((enc_edges, LANES), jnp.int16),
+        pltpu.VMEM((dec_edges, LANES), jnp.int16),
+        pltpu.VMEM((cells, features), F32),
         pltpu.VMEM((slots, features), BF16),
+        pltpu.VMEM((3, peers, 16, LANES), BF16),
         pltpu.VMEM((6, peers, 16, LANES), BF16),
-        pltpu.VMEM((6, peers, 16, LANES), BF16),
-        pltpu.VMEM((tile, features), F32),
-        pltpu.VMEM((tile, features), BF16),
-        pltpu.VMEM((tile, features), BF16),
-        pltpu.VMEM((enc_edges + tile, features), BF16),
-        pltpu.VMEM((enc_edges + tile, features), F32),
+        pltpu.VMEM((2, tile, features), F32),
+        pltpu.VMEM((2, tile, features), BF16),
+        pltpu.VMEM((2, tile, features), BF16),
+        pltpu.VMEM((enc_edges + 2 * tile, features), BF16),
+        pltpu.VMEM((enc_edges + 2 * tile, features), F32),
         pltpu.VMEM((enc_edges, features), F32),
         pltpu.VMEM((enc_edges, 1), F32),
         pltpu.VMEM((dec_edges, features), BF16),
         pltpu.VMEM((cells, features), F32),
         pltpu.VMEM((mesh_rows, features), BF16),
-        pltpu.VMEM((mesh_rows, features), F32),
         pltpu.VMEM((sz.chunk, features), F32),
         pltpu.VMEM((3 * features, features), F32),
-        pltpu.VMEM((3, 8, features), F32),
-        *[pltpu.VMEM((sz.near, own, 16, LANES), kind) for kind in PART_WIRE],
-        *[pltpu.VMEM((sz.near, own, 16, LANES), kind) for kind in PART_WIRE],
-        *[pltpu.VMEM((sz.active, sz.piece, 16, LANES), F32) for kind in PART_WIRE],
-        *[pltpu.VMEM((sz.far, sz.piece, 16, LANES), F32) for kind in PART_WIRE],
-        *[pltpu.VMEM((sz.active, sz.piece, 16, LANES), kind) for kind in PART_WIRE],
-        *[pltpu.VMEM((sz.near, sz.active, sz.piece, 16, LANES), kind) for kind in PART_WIRE],
-        *[pltpu.VMEM((sz.far, sz.piece, 16, LANES), kind) for kind in PART_WIRE],
-        dma((7,)), dma((7,)), dma((2, 4)), dma((2, 4)),
+        pltpu.VMEM((2, 3, 8, features), F32),
+        *[pltpu.VMEM(shape, F32) for shape in ((2, sz.half, 16, LANES), (sz.half, 16, LANES)) for _ in range(2)],
+        *[pltpu.VMEM((sz.near[l], own[l] if sz.near[l] > 1 else 1, 16, LANES), PART_SUM_WIRE[l]) for l in range(2)],
+        *[pltpu.VMEM((sz.near[l], own[l] if sz.near[l] > 1 else 1, 16, LANES), PART_SUM_WIRE[l]) for l in range(2)],
+        *[pltpu.VMEM((sz.active[l], sz.piece[l], 16, LANES), far_wire[l]) for l in range(2)],
+        *[pltpu.VMEM((sz.far[l], sz.piece[l], 16, LANES), far_wire[l]) for l in range(2)],
+        *[pltpu.VMEM((sz.active[l], sz.piece[l], 16, LANES), PART_WIRE[l]) for l in range(2)],
+        *[pltpu.VMEM((sz.near[l], sz.active[l], sz.piece[l], 16, LANES), PART_WIRE[l]) for l in range(2)],
+        *[pltpu.VMEM((2, sz.near[l], sz.active[l], sz.piece[l], 16, LANES), PART_WIRE[l]) for l in range(2)],
+        *[pltpu.VMEM((sz.far[l], sz.piece[l], 16, LANES), PART_WIRE[l]) for l in range(2)],
+        dma((7,)), dma((7,)), dma((2, 6)), dma((2, 6)),
     ]
     made = tuple(
         pl.pallas_call(

time: 163 us -> 151 us (0.926)
  Pallas kernels: 160 us -> 147 us
    pallas_call x1, Pallas kernels: 156 us -> 143 us  [per_device(): pl.pallas_call(functools.partial(kernel, sz), out_shape=outs, in_specs=[v...]
where the time goes in v4:
time: 151 us; the launch traced here: 150 us
  Pallas kernels  147 us (97%)
    pallas_call x1, Pallas kernels, per_device(): pl.pallas_call(functools.partial(kernel, sz), out_shape=outs, in_specs=[v...  143 us
    pallas_call x1, Pallas kernels, per_device(): pl.pallas_call(functools.partial(hand_over, len(made)), out_shape=outs, i...  4.07 us

profile of v4, /device:TPU:1, one launch (start us, length us, event | category | flops | bytes accessed | tf_op | source)
XLA Modules:
  0.0 150.3 jit_solution(1581979379306199857)
XLA Ops:
  0.6 0.8 copy.20
  1.4 0.7 fusion
  2.2 0.6 pad.4
  2.8 143.3 %shard_map.180 = (f32[2048,256]{1,0:T(8,128)}, f32[1536,256]{1,0:T(8,128)}, f32[2,512,256]{2,1,0:T(8,128)}, f32[2,256,256]{2,1,0:T(8,128)}, f32[2,256]{1,0:T(2,1...) custom-call(bf16[2048,256]{1,0:T(8,128)(2,1)} %grid_ref.1, bf16[1536,256]{1,0:T(8,128)(2,1)} %lat_ref.1, ...), custom_call_target="tpu_custom_call" | custom-call | tf_op jit(solution)/shard_map/pallas_call | solution.py:695
  146.1 4.1 %shard_map.181 = (f32[2048,256]{1,0:T(8,128)}, f32[1536,256]{1,0:T(8,128)}, f32[2,512,256]{2,1,0:T(8,128)}, f32[2,256,256]{2,1,0:T(8,128)}, f32[2,256]{1,0:T(2,1...) custom-call(f32[2048,256]{1,0:T(8,128)} %get-tuple-element.14.refs_0_, f32[1536,256]{1,0:T(8,128)} %get-tuple-element.15.refs_1_, ...), custom_call_target="tpu_custom_call" | custom-call | tf_op jit(solution)/shard_map/pallas_call | solution.py:712

commit v5 on v4

--- a/solution.py
+++ b/solution.py
@@ -70,11 +70,11 @@
 def kernel(
     sz,
     grid_ref, lat_ref, cot_ref, mesh_cot_ref, w1_ref, w2_ref, bias_ref, gain_ref, shift_ref,
-    ask_ref, enc_row_ref, dec_row_ref,
+    request_ref, count_ref, enc_row_ref, dec_row_ref,
     grid_out, mesh_out, w1_out, w2_out, bias_out, gain_out, shift_out,
-    asked, ask_col, ask_row, enc_row, dec_row, enc_col, dec_col, base, table, stage, landed,
+    asked, asking, ask_col, ask_row, enc_row, dec_row, enc_col, dec_col, base, table, stage, landed,
     pre, xm, outer_low, hidden, deriv, normed, invstd, edge_low,
-    cell_sum, mid, slot_sum, parts, part_vec,
+    cell_sum, cot_asked, slot_sum, parts, part_vec,
     pair_src_enc, pair_src_dec, pair_land_enc, pair_land_dec, near_src_enc, near_src_dec,
     near_land_enc, near_land_dec, far_src_enc, far_src_dec, far_land_enc, far_land_dec,
     far_sum_enc, far_sum_dec, near_sum_enc, near_sum_dec, pair_sum_enc, pair_sum_dec, far_wide_enc, far_wide_dec,
@@ -129,6 +129,7 @@
             bases[layer][span] = dot(grid_ref[span], w1_ref[layer, :256]) + bias_ref[layer:layer + 1]
 
         loop(sz.cells // tile, cell_part)
+    def local_columns(layer):
         for which in range(sz.fanout[layer]):
             turned = row_refs[layer][which:which + 1].astype(F32) - (8 * me).astype(F32)
             turned = jnp.where(turned < 0.0, turned + slots, turned)
@@ -148,20 +149,28 @@
         return carry
 
     lax.fori_loop(1, peers, greet, 0, unroll=8)
+    square = (peers, peers)
+    same = lax.broadcasted_iota(jnp.int32, square, 0) == lax.broadcasted_iota(jnp.int32, square, 1)
+    live = jnp.broadcast_to(count_ref[...].astype(F32), square)
+    live = jnp.sum(jnp.where(same, live, 0.0), axis=1, keepdims=True).astype(jnp.int32)
+    slot = lax.broadcasted_iota(jnp.int32, (peers, 8), 1)
+    asking[...] = jnp.full(asking.shape, -1, jnp.int32)
+    asking[:, 0, :8] = jnp.where(slot < live, request_ref[...], -1)
     local_work(ENC)
+    local_columns(ENC)
     pl.semaphore_wait(barrier, peers - 1)
 
     def ask(step, carry):
         peer = lax.rem(me + step, peers)
         pltpu.make_async_remote_copy(
-            src_ref=ask_ref.at[peer], dst_ref=asked.at[peers - step],
+            src_ref=asking.at[peer], dst_ref=asked.at[peers - step],
             send_sem=send_sem.at[0], recv_sem=recv_sem.at[0],
             device_id=place(peer), device_id_type=pl.DeviceIdType.MESH,
         ).start()
         return carry
 
     lax.fori_loop(1, peers, ask, 0, unroll=8)
-    asked[0] = ask_ref[me]
+    asked[0] = asking[me]
 
     def send(phase, start, stop):
         def one(step, carry):
@@ -183,6 +192,8 @@
     def wait_rows(phase):
         wait(recv_sem.at[phase], landed.at[phase - 1], peers - 1)
         wait(send_sem.at[phase], landed.at[phase - 1], peers - 1)
+
+    local_columns(DEC)
 
     wait(recv_sem.at[0], asked, peers - 1)
     wide = asked[...].astype(F32)
@@ -196,15 +207,29 @@
         square = jnp.transpose(picked[index * LANES:(index + 1) * LANES])
         ask_row[:, index * LANES:(index + 1) * LANES] = square[:8].astype(jnp.int32)
 
-    def serve(phase, source):
+    def asked_rows(start, source):
+        column = ask_col[start:start + chunk]
+        lanes = lax.broadcasted_iota(jnp.int32, (chunk, LANES), 1)
+        chosen = jnp.concatenate(
+            [one_hot(column == lanes + first) for first in range(0, sz.mesh_rows, LANES)], axis=1
+        )[:, :sz.mesh_rows]
+        return dot(chosen, source[...])
+
+    def serve(phase, make):
         for start in range(0, slots, chunk):
-            column = ask_col[start:start + chunk]
-            lanes = lax.broadcasted_iota(jnp.int32, (chunk, LANES), 1)
-            chosen = jnp.concatenate(
-                [one_hot(column == lanes + first) for first in range(0, sz.mesh_rows, LANES)], axis=1
-            )[:, :sz.mesh_rows]
-            stage[(phase - 1) % 3, start // 8:(start + chunk) // 8] = to_blocks(dot(chosen, source[...]))
+            stage[(phase - 1) % 3, start // 8:(start + chunk) // 8] = to_blocks(make(start))
             send(phase, start // 8, (start + chunk) // 8)
+
+    def returned_rows(start):
+        column = ask_col[start:start + chunk]
+        same = jnp.concatenate(
+            [
+                one_hot(column == jnp.broadcast_to(ask_row[0:1, first:first + LANES], (chunk, LANES)))
+                for first in range(0, slots, LANES)
+            ],
+            axis=1,
+        )
+        return dot(same, table[...])
 
     def fetch(phase):
         wait_rows(phase)
@@ -499,7 +524,9 @@
         for which, out in enumerate((bias_out, gain_out, shift_out)):
             out[layer:layer + 1] = jnp.concatenate([last[2 * which:2 * which + 1], last[2 * which + 1:2 * which + 2]], axis=1)
 
-    serve(1, lat_ref)
+    serve(1, lambda start: asked_rows(start, lat_ref))
+    for start in range(0, slots, chunk):
+        cot_asked[start:start + chunk] = asked_rows(start, mesh_cot_ref).astype(BF16)
     local_work(DEC)
     clear_parts()
     fetch(1)
@@ -526,12 +553,7 @@
 
     fetch(2)
 
-    def make_mid(index):
-        span = rows_of(index, sz.own_rows)
-        mid[span] = (lat_ref[span].astype(F32) + returned(2, index * sz.own_rows, span)).astype(BF16)
-
-    loop(sz.mesh_rows // sz.own_rows, make_mid)
-    serve(3, mid)
+    serve(3, lambda start: from_blocks(stage[0, start // 8:(start + chunk) // 8]) + returned_rows(start))
     fetch(3)
 
     def decode(index, side):
@@ -560,12 +582,10 @@
 
     def make_mid_grad(index):
         span = rows_of(index, sz.own_rows)
-        total = mesh_cot_ref[span].astype(F32) + returned(4, index * sz.own_rows, span)
-        mesh_out[span] = total
-        mid[span] = total.astype(BF16)
-
+        mesh_out[span] = mesh_cot_ref[span].astype(F32) + returned(4, index * sz.own_rows, span)
+
+    serve(5, lambda start: cot_asked[start:start + chunk].astype(F32) + returned_rows(start))
     loop(sz.mesh_rows // sz.own_rows, make_mid_grad)
-    serve(5, mid)
     clear_parts()
     reduce_pair(DEC)
     fetch(5)
@@ -640,9 +660,6 @@
     mesh_rows = mesh_node_latents.shape[0]
     sz = Sizes(slabs, bricks, cells, mesh_rows, enc_slots.shape[0], dec_slots.shape[0])
     peers, slots, tile = sz.peers, sz.slots, sz.tile
-    positions = lax.broadcasted_iota(jnp.int32, (peers, 8), 1)
-    asking = jnp.where(positions < counts.reshape(peers, 1), requests, -1)
-    asking = jnp.pad(asking, ((0, 0), (0, LANES - 8))).reshape(peers, 1, LANES)
     enc_edges, dec_edges = sz.fanout[ENC] * cells, sz.fanout[DEC] * cells
     vmem = pl.BlockSpec(memory_space=pltpu.VMEM)
     outs = [
@@ -656,6 +673,7 @@
     own = [sz.active[l] * sz.piece[l] for l in range(2)]
     far_wire = [F32 if sz.near[l] > 1 else PART_SUM_WIRE[l] for l in range(2)]
     scratch = [
+        pltpu.VMEM((peers, 1, LANES), jnp.int32),
         pltpu.VMEM((peers, 1, LANES), jnp.int32),
         pltpu.VMEM((slots, LANES), jnp.int32),
         pltpu.VMEM((8, slots), jnp.int32),
@@ -676,7 +694,7 @@
         pltpu.VMEM((enc_edges, 1), F32),
         pltpu.VMEM((dec_edges, features), BF16),
         pltpu.VMEM((cells, features), F32),
-        pltpu.VMEM((mesh_rows, features), BF16),
+        pltpu.VMEM((slots, features), BF16),
         pltpu.VMEM((sz.chunk, features), F32),
         pltpu.VMEM((3 * features, features), F32),
         pltpu.VMEM((2, 3, 8, features), F32),
@@ -695,7 +713,7 @@
         pl.pallas_call(
             functools.partial(kernel, sz),
             out_shape=outs,
-            in_specs=[vmem] * 12,
+            in_specs=[vmem] * 13,
             out_specs=[vmem] * 7,
             scratch_shapes=scratch,
             compiler_params=pltpu.CompilerParams(
@@ -703,7 +721,7 @@
             ),
         )(
             grid_latent, mesh_node_latents, grid_cot, mesh_cotangent, w_first, w_second,
-            biases, ln_gain, ln_shift, asking,
+            biases, ln_gain, ln_shift, requests, counts,
             enc_slots, dec_slots,
         )
     )

time: 151 us -> 146 us (0.967)
  Pallas kernels: 147 us -> 144 us
    pallas_call x1, Pallas kernels: 143 us -> 140 us  [per_device(): pl.pallas_call(functools.partial(kernel, sz), out_shape=outs, in_specs=[v...]
where the time goes in v5:
time: 146 us
  Pallas kernels  144 us (99%)
    pallas_call x1, Pallas kernels, per_device(): pl.pallas_call(functools.partial(kernel, sz), out_shape=outs, in_specs=[v...  140 us
    pallas_call x1, Pallas kernels, per_device(): pl.pallas_call(functools.partial(hand_over, len(made)), out_shape=outs, i...  4.07 us

profile of v5, /device:TPU:1, one launch (start us, length us, event | category | flops | bytes accessed | tf_op | source)
XLA Modules:
  0.0 146.2 jit_solution(3702374681455625759)
XLA Ops:
  0.6 1.4 copy.20.request_ref
  2.0 139.9 %shard_map.180 = (f32[2048,256]{1,0:T(8,128)}, f32[1536,256]{1,0:T(8,128)}, f32[2,512,256]{2,1,0:T(8,128)}, f32[2,256,256]{2,1,0:T(8,128)}, f32[2,256]{1,0:T(2,1...) custom-call(bf16[2048,256]{1,0:T(8,128)(2,1)} %grid_ref.1, bf16[1536,256]{1,0:T(8,128)(2,1)} %lat_ref.1, ...), custom_call_target="tpu_custom_call" | custom-call | tf_op jit(solution)/shard_map/pallas_call | solution.py:713
  142.0 4.1 %shard_map.181 = (f32[2048,256]{1,0:T(8,128)}, f32[1536,256]{1,0:T(8,128)}, f32[2,512,256]{2,1,0:T(8,128)}, f32[2,256,256]{2,1,0:T(8,128)}, f32[2,256]{1,0:T(2,1...) custom-call(f32[2048,256]{1,0:T(8,128)} %get-tuple-element.14.refs_0_, f32[1536,256]{1,0:T(8,128)} %get-tuple-element.15.refs_1_, ...), custom_call_target="tpu_custom_call" | custom-call | tf_op jit(solution)/shard_map/pallas_call | solution.py:730

commit v6 on v5

--- a/solution.py
+++ b/solution.py
@@ -71,7 +71,8 @@
     sz,
     grid_ref, lat_ref, cot_ref, mesh_cot_ref, w1_ref, w2_ref, bias_ref, gain_ref, shift_ref,
     request_ref, count_ref, enc_row_ref, dec_row_ref,
-    grid_out, mesh_out, w1_out, w2_out, bias_out, gain_out, shift_out,
+    grid_hbm, mesh_hbm, w1_hbm, w2_hbm, bias_out, gain_out, shift_out,
+    grid_out, mesh_out, w1_out, w2_out, out_sem,
     asked, asking, ask_col, ask_row, enc_row, dec_row, enc_col, dec_col, base, table, stage, landed,
     pre, xm, outer_low, hidden, deriv, normed, invstd, edge_low,
     cell_sum, cot_asked, slot_sum, parts, part_vec,
@@ -259,6 +260,13 @@
             slot_sum[...] += dot(one_hot(row == sub), edge_low[rows_of(index, tile)])
 
         loop(sz.fanout[layer] * sz.cells // tile, add)
+
+    def leave(which):
+        pairs = (
+            (grid_out, grid_hbm), (mesh_out, mesh_hbm), (w1_out.at[DEC], w1_hbm.at[DEC]), (w2_out.at[DEC], w2_hbm.at[DEC]),
+            (w1_out.at[ENC], w1_hbm.at[ENC]), (w2_out.at[ENC], w2_hbm.at[ENC]),
+        )
+        return pltpu.make_async_copy(*pairs[which], out_sem.at[which])
 
     def cells_of(layer, index):
         return lax.rem(index, sz.cells // tile) * tile
@@ -612,6 +620,7 @@
     in_pairs(tiles - tiles // 2, lambda index, side: encode_back(index + tiles // 2, side))
     spread_near(DEC)
     cell_back(ENC)
+    leave(0).start()
     table[...] = from_blocks(landed[0]).astype(BF16)
     send_slot_grads(ENC, 6)
     send_parts(ENC)
@@ -621,6 +630,8 @@
         if start == 0:
             reduce_pair(ENC)
     finish_parts(DEC)
+    leave(2).start()
+    leave(3).start()
     fetch(6)
     reduce_near(ENC)
     reduce_far(ENC)
@@ -632,8 +643,13 @@
     loop(sz.mesh_rows // sz.own_rows - 1, make_mesh_out)
     spread_near(ENC)
     make_mesh_out(sz.mesh_rows // sz.own_rows - 1)
+    leave(1).start()
     spread_pair(ENC)
     finish_parts(ENC)
+    leave(4).start()
+    leave(5).start()
+    for which in range(6):
+        leave(which).wait()
     wait(send_sem.at[0], asked, peers - 1)
 
 
@@ -662,6 +678,7 @@
     peers, slots, tile = sz.peers, sz.slots, sz.tile
     enc_edges, dec_edges = sz.fanout[ENC] * cells, sz.fanout[DEC] * cells
     vmem = pl.BlockSpec(memory_space=pltpu.VMEM)
+    anywhere = pl.BlockSpec(memory_space=pl.ANY)
     outs = [
         jax.ShapeDtypeStruct(shape, F32)
         for shape in (
@@ -673,6 +690,7 @@
     own = [sz.active[l] * sz.piece[l] for l in range(2)]
     far_wire = [F32 if sz.near[l] > 1 else PART_SUM_WIRE[l] for l in range(2)]
     scratch = [
+        *[pltpu.VMEM(out.shape, F32) for out in outs[:4]], dma((6,)),
         pltpu.VMEM((peers, 1, LANES), jnp.int32),
         pltpu.VMEM((peers, 1, LANES), jnp.int32),
         pltpu.VMEM((slots, LANES), jnp.int32),
@@ -714,7 +732,7 @@
             functools.partial(kernel, sz),
             out_shape=outs,
             in_specs=[vmem] * 13,
-            out_specs=[vmem] * 7,
+            out_specs=[anywhere] * 4 + [vmem] * 3,
             scratch_shapes=scratch,
             compiler_params=pltpu.CompilerParams(
                 collective_id=1, has_side_effects=True, vmem_limit_bytes=62 << 20
@@ -725,7 +743,6 @@
             enc_slots, dec_slots,
         )
     )
-    anywhere = pl.BlockSpec(memory_space=pl.ANY)
     return tuple(
         pl.pallas_call(
             functools.partial(hand_over, len(made)),

time: 146 us -> 145 us (level)
  no operation moved by 1% of the time
where the time goes in v6:
time: 145 us
  Pallas kernels  143 us (99%)
    pallas_call x1, Pallas kernels, per_device(): pl.pallas_call(functools.partial(kernel, sz), out_shape=outs, in_specs=[v...  139 us
    pallas_call x1, Pallas kernels, per_device(): pl.pallas_call(functools.partial(hand_over, len(made)), out_shape=outs, i...  4.07 us

profile of v6, /device:TPU:1, one launch (start us, length us, event | category | flops | bytes accessed | tf_op | source)
XLA Modules:
  0.0 145.2 jit_solution(17188579761763888982)
XLA Ops:
  0.6 1.4 copy.20.request_ref
  2.0 138.9 %shard_map.180 = (f32[2048,256]{1,0:T(8,128)}, f32[1536,256]{1,0:T(8,128)}, f32[2,512,256]{2,1,0:T(8,128)}, f32[2,256,256]{2,1,0:T(8,128)}, f32[2,256]{1,0:T(2,1...) custom-call(bf16[2048,256]{1,0:T(8,128)(2,1)} %grid_ref.1, bf16[1536,256]{1,0:T(8,128)(2,1)} %lat_ref.1, ...), custom_call_target="tpu_custom_call" | custom-call | tf_op jit(solution)/shard_map/pallas_call | solution.py:731
  141.0 4.1 %shard_map.181 = (f32[2048,256]{1,0:T(8,128)}, f32[1536,256]{1,0:T(8,128)}, f32[2,512,256]{2,1,0:T(8,128)}, f32[2,256,256]{2,1,0:T(8,128)}, f32[2,256]{1,0:T(2,1...) custom-call(f32[2048,256]{1,0:T(8,128)} %get-tuple-element.14.refs_0_, f32[1536,256]{1,0:T(8,128)} %get-tuple-element.15.refs_1_, ...), custom_call_target="tpu_custom_call" | custom-call | tf_op jit(solution)/shard_map/pallas_call | solution.py:747
